TPU v7x, 512 devices: a whole 4x8x8 slice. The times are simulated.
512 devices in a mesh: ckpt: 4 (over x), vocab: 128 (over z, y, core).
Axes of the slice: x: 4, y: 8, z: 8, core: 2. Of those that a mesh axis runs over, the one named last changes fastest.
Arguments:
- token_ids: int32 [16384], P('vocab'), may hold values from 0 to 16383, as said below
- grad_values: bfloat16 [4, 16384, 8192], P('ckpt', 'vocab'), may hold values from -6 to 6
- grad_scales: float32 [4, 64, 16384], P('ckpt', None, 'vocab'), may hold values from 0.3 to 3
- tables: bfloat16 [4, 16384, 8192], P('ckpt', 'vocab'), may hold values from -6 to 6
Outputs:
- merged: bfloat16 [16384, 8192], P('vocab', 'ckpt')
Inputs may be any that keep to these rules, and one draw needn't show every extreme that they name: The owner of a token is token_ids // 128. Among the 128 tokens of each index of vocab, exactly 64 owners appear, each with exactly 2 tokens; one owner appears in every index's tokens. Ids repeat and some owners are far more frequent than others.
All inputs are finite; a program needn't handle non-finite values.
Results may differ from a plain program's by a relative error of at most 0.018.
Values may be sent and summed in bfloat16 or wider, within the bound.
No kernel may reach another device: no remote copies, remote signals or barrier semaphores. Data moves between devices by JAX's collectives and lax.ppermute only.
A program may use at most 64 MiB of HBM per device.

v0:
```python
import jax
import jax.numpy as jnp
from jax import lax
from jax.sharding import PartitionSpec as P

BLK = 128


prior_weight = 1.0


def per_device(token_ids, grad_values, grad_scales, tables):
    groups = lax.axis_size("vocab")
    rows = tables.shape[1]
    width = tables.shape[2]
    count = token_ids.shape[0]
    capacity = 2 * count // groups
    owner = token_ids // rows
    same = owner[:, None] == owner[None, :]
    before = lax.broadcasted_iota(jnp.int32, (count, count), 0) < lax.broadcasted_iota(
        jnp.int32, (count, count), 1
    )
    rank = jnp.sum((same & before).astype(jnp.int32), axis=0)
    slot = owner * capacity + rank
    match = lax.broadcasted_iota(jnp.int32, (groups * capacity, count), 0) == slot[None, :]
    scales = grad_scales[0].T
    grads = (
        grad_values[0].astype(jnp.float32).reshape(count, width // BLK, BLK) * scales[:, :, None]
    )
    squares = (grads * grads).reshape(count, width).astype(jnp.bfloat16)
    placed = jnp.dot(match.astype(jnp.bfloat16), squares, preferred_element_type=jnp.float32)
    buffer = placed.astype(jnp.bfloat16).reshape(groups, capacity, width)
    local_rows = token_ids % rows
    row_tags = (
        jnp.sum(jnp.where(match, local_rows[None, :], 0), axis=1)
        .astype(jnp.bfloat16)
        .reshape(groups, capacity)
    )
    arrived, arrived_rows = (
        lax.all_to_all(buffer, "vocab", split_axis=0, concat_axis=0, tiled=True),
        lax.all_to_all(row_tags, "vocab", split_axis=0, concat_axis=0, tiled=True),
    )
    flat_rows = arrived_rows.reshape(groups * capacity).astype(jnp.int32)
    selector = (
        lax.broadcasted_iota(jnp.int32, (rows, groups * capacity), 0) == flat_rows[None, :]
    ).astype(jnp.bfloat16)
    fisher = jnp.dot(
        selector, arrived.reshape(groups * capacity, width), preferred_element_type=jnp.float32
    )
    weight = (fisher + prior_weight).astype(jnp.bfloat16)
    term = (weight.astype(jnp.float32) * tables[0].astype(jnp.float32)).astype(jnp.bfloat16)
    numer, denom = (
        lax.psum_scatter(term, "ckpt", scatter_dimension=1, tiled=True).astype(jnp.float32),
        lax.psum_scatter(weight, "ckpt", scatter_dimension=1, tiled=True).astype(jnp.float32),
    )
    return (numer / denom).astype(jnp.bfloat16)


def solution(mesh):
    return jax.shard_map(
        per_device,
        mesh=mesh,
        in_specs=(
            P("vocab"),
            P("ckpt", "vocab", None),
            P("ckpt", None, "vocab"),
            P("ckpt", "vocab", None),
        ),
        out_specs=P("vocab", "ckpt"),
        check_vma=False,
    )
```

profile of v0, /device:TPU:1, one launch (start us, length us, event | category | flops | bytes accessed | tf_op | source)
XLA Modules:
  0.0 249.9 jit_solution(2180431784331541404)
XLA Ops:
  6.5 0.0 copy-start
  6.5 0.8 and_select_fusion
  7.4 0.1 convert_reduce_fusion.1
  7.5 0.1 select_reduce_fusion
  7.6 0.8 convert_element_type.87
  8.4 18.4 %all-to-all-start = ((bf16[128,1,2]{2,1,0:T(2,128)(2,1)}), bf16[128,1,2]{2,1,0:T(2,128)(2,1)S(1)}, u32[]{:S(2)}, u32[]{:S(2)}) async-start(bf16[128,1,2]{2,1,0:T(2,128)(2,1)} %convert_element_type.87), calls=%async_computation | async-start | bytes 131072 | tf_op jit(solution)/shard_map/all_to_all | solution.py:41
  26.8 0.8 copy.10
  27.7 1.1 mul.26
  28.8 0.0 copy-done
  28.8 5.1 %convolution_convert_fusion = bf16[256,8192]{1,0:T(8,128)(2,1)} fusion(f32[16,8,64,128]{3,2,1,0:T(8,128)S(1)} %bitcast.21, bf16[1,128,8192]{2,1,0:T(8,128)(2,1)S(1)} %copy-done, s32[128]{0:T(128)S(1)} %multiply_add_fusion), kind=kOutput, calls=%fused_computation | convolution fusion | flops 543195136 | bytes 10486272 | tf_op jit(solution)/shard_map/dot_general | solution.py:31
  33.9 7.6 %reshape.44 = bf16[128,2,8192]{2,1,0:T(2,128)(2,1)} reshape(bf16[256,8192]{1,0:T(8,128)(2,1)} %convolution_convert_fusion) | data formatting | bytes 8388608 | tf_op jit(solution)/shard_map/reshape | solution.py:32
  41.5 0.0 all-to-all-done
  41.6 14.2 %all-to-all-start.1 = ((bf16[128,2,8192]{2,1,0:T(2,128)(2,1)}), bf16[128,2,8192]{2,1,0:T(2,128)(2,1)}, u32[]{:S(2)}, u32[]{:S(2)}) async-start(bf16[128,2,8192]{2,1,0:T(2,128)(2,1)} %reshape.44), calls=%async_computation.1 | async-start | bytes 8388608 | tf_op jit(solution)/shard_map/all_to_all | solution.py:40
  55.7 0.0 reduce-scatter.3.cloned.1.call-start
  55.8 0.2 convert_reduce_fusion
  56.0 0.1 reshape.46
  56.2 0.0 copy-start.1
  56.2 96.1 %all-to-all-done.1 = bf16[128,2,8192]{2,1,0:T(2,128)(2,1)} async-done(((bf16[128,2,8192]{2,1,0:T(2,128)(2,1)}), bf16[128,2,8192]{2,1,0:T(2,128)(2,1)}, u32[]{:S(2)}, u32[]{:S(2)}) %all-to-all-start.1) | async-done | bytes 4194336 | tf_op jit(solution)/shard_map/all_to_all | solution.py:40
  152.3 7.2 %reshape.45 = bf16[256,8192]{1,0:T(8,128)(2,1)} reshape(bf16[128,2,8192]{2,1,0:T(2,128)(2,1)} %all-to-all-done.1) | data formatting | bytes 8388608 | tf_op jit(solution)/shard_map/reshape | solution.py:48
  159.5 0.0 copy-done.1
  159.5 5.1 %fusion.3 = (bf16[128,8192]{1,0:T(8,128)(2,1)}, bf16[128,8192]{1,0:T(8,128)(2,1)}) fusion(bf16[1,128,8192]{2,1,0:T(8,128)(2,1)S(1)} %copy-done.1, bf16[256,8192]{1,0:T(8,128)(2,1)} %reshape.45, s32[256]{0:T(256)S(1)} %reshape.46), kind=kOutput, calls=%fused_computation.7 | convolution fusion | flops 543195136 | bytes 10486784 | tf_op jit(solution)/shard_map/dot_general | solution.py:47
  164.6 0.0 reduce-scatter.3.cloned.1.call-update
  164.6 0.0 reduce-scatter.5.cloned.1.call-start
  164.7 0.7 reduce-scatter.5.cloned.1.call-update
  165.4 37.7 %reduce-scatter.3.cloned.1.call-done = bf16[128,2048]{1,0:T(8,128)(2,1)} async-done(((bf16[128,8192]{1,0:T(8,128)(2,1)}), bf16[128,2048]{1,0:T(8,128)(2,1)}) %reduce-scatter.3.cloned.1.call-update) | async-done | bytes 524304 | tf_op jit(solution)/shard_map/reduce_scatter | solution.py:53
  203.0 37.9 %reduce-scatter.5.cloned.1.call-done = bf16[128,2048]{1,0:T(8,128)(2,1)} async-done(((bf16[128,8192]{1,0:T(8,128)(2,1)}), bf16[128,2048]{1,0:T(8,128)(2,1)}) %reduce-scatter.5.cloned.1.call-update) | async-done | bytes 524304 | tf_op jit(solution)/shard_map/reduce_scatter | solution.py:54
  240.9 2.2 divide_convert_fusion
  (2 shorter events, 0.0 us)
Async XLA Ops:
  6.5 22.3 %copy-start = (bf16[1,128,8192]{2,1,0:T(8,128)(2,1)S(1)}, bf16[1,128,8192]{2,1,0:T(8,128)(2,1)}, u32[]{:S(2)}) copy-start(bf16[1,128,8192]{2,1,0:T(8,128)(2,1)} %param.5) | copy-start | bytes 6291460
  8.4 33.2 %all-to-all-start = ((bf16[128,1,2]{2,1,0:T(2,128)(2,1)}), bf16[128,1,2]{2,1,0:T(2,128)(2,1)S(1)}, u32[]{:S(2)}, u32[]{:S(2)}) async-start(bf16[128,1,2]{2,1,0:T(2,128)(2,1)} %convert_element_type.87), calls=%async_computation | async-start | bytes 131072 | tf_op jit(solution)/shard_map/all_to_all | solution.py:41
  41.6 110.7 %all-to-all-start.1 = ((bf16[128,2,8192]{2,1,0:T(2,128)(2,1)}), bf16[128,2,8192]{2,1,0:T(2,128)(2,1)}, u32[]{:S(2)}, u32[]{:S(2)}) async-start(bf16[128,2,8192]{2,1,0:T(2,128)(2,1)} %reshape.44), calls=%async_computation.1 | async-start | bytes 8388608 | tf_op jit(solution)/shard_map/all_to_all | solution.py:40
  55.7 147.3 %reduce-scatter.3.cloned.1.call-start = ((), (), s32[]{:S(2)}) async-start(), calls=%async_computation.4 | async-start | bytes 2621440 | tf_op jit(solution)/shard_map/reduce_scatter | solution.py:53
  56.2 103.4 %copy-start.1 = (bf16[1,128,8192]{2,1,0:T(8,128)(2,1)S(1)}, bf16[1,128,8192]{2,1,0:T(8,128)(2,1)}, u32[]{:S(2)}) copy-start(bf16[1,128,8192]{2,1,0:T(8,128)(2,1)} %param.7) | copy-start | bytes 6291460
  164.6 76.3 %reduce-scatter.5.cloned.1.call-start = ((), (), s32[]{:S(2)}) async-start(), calls=%async_computation.5 | async-start | bytes 2621440 | tf_op jit(solution)/shard_map/reduce_scatter | solution.py:54
Sparse Core Ops, SparseCore 0:
  164.8 38.2 reduce-scatter.2
  206.1 34.7 reduce-scatter.4
where the time goes:
time: 251 us; the launch traced here: 250 us
  waiting for transfers between devices  172 us (69%)
  starting transfers between devices  32.7 us (13%)
  local copies, waits for them, and re-layouts  17.8 us (7%)
  between operations  13.5 us (5%)
  matrix products  10.2 us (4%)
  other arithmetic  3.41 us (1%)
    all_to_all x1, waiting for transfers between devices, per_device(): lax.all_to_all(buffer, 'vocab', split_axis=0, concat_axis=0, tiled=True)  96.1 us
    reduce_scatter x1, waiting for transfers between devices, per_device(): lax.psum_scatter(weight, 'ckpt', scatter_dimension=1, tiled=True)  37.9 us
    reduce_scatter x1, waiting for transfers between devices, per_device(): lax.psum_scatter(term, 'ckpt', scatter_dimension=1, tiled=True)  37.7 us
    all_to_all x1, starting transfers between devices, per_device(): lax.all_to_all(row_tags, 'vocab', split_axis=0, concat_axis=0, tiled=True)  18.4 us
    all_to_all x1, starting transfers between devices, per_device(): lax.all_to_all(buffer, 'vocab', split_axis=0, concat_axis=0, tiled=True)  14.2 us
    reshape x1, local copies, waits for them, and re-layouts, per_device(): buffer = placed.astype(jnp.bfloat16).reshape(groups, capacity, width)  7.62 us
    reshape x1, local copies, waits for them, and re-layouts, per_device(): arrived.reshape(groups * capacity, width)  7.21 us
    dot_general x1, matrix products, per_device(): jnp.dot(selector, arrived.reshape(groups * capacity, width), preferred_el...  5.11 us
  transfers between devices with their start and end apart: 4, of which 3 were waited for; matrix products, arithmetic and copies ran while one was open for 6% of the time, Pallas kernels for 0%

commit v1 on v0

v1 whole, which is shorter than its diff:
```python
import functools

import jax
import jax.numpy as jnp
from jax import lax
from jax.experimental import pallas as pl
from jax.experimental.pallas import tpu as pltpu
from jax.sharding import PartitionSpec as P

BLK = 128
CAP = 2
SUB = 4

prior_weight = 1.0


def place_kernel(slot_ref, scales_ref, grads_ref, out_ref, match_ref):
    count = grads_ref.shape[0]
    quarter = grads_ref.shape[1]
    rows = out_ref.shape[0]
    cols = quarter // SUB

    @pl.when(pl.program_id(0) == 0)
    def _():
        slot = slot_ref[...]
        for b in range(SUB):
            target = (slot // CAP) * (CAP * SUB) + (slot % CAP) * SUB + b
            hit = lax.broadcasted_iota(jnp.int32, (rows, count), 0) == target
            match_ref[:, b * count : (b + 1) * count] = jnp.where(hit, 1.0, 0.0).astype(jnp.bfloat16)

    scales = scales_ref[...]
    blocks = scales.shape[0]
    scales = jnp.concatenate([scales, jnp.zeros((count - blocks, count), jnp.float32)], axis=0).T
    per = cols // BLK
    stacked = []
    for b in range(SUB):
        pieces = []
        for j in range(b * per, (b + 1) * per):
            grads = grads_ref[:, j * BLK : (j + 1) * BLK].astype(jnp.float32) * scales[:, j : j + 1]
            pieces.append((grads * grads).astype(jnp.bfloat16))
        stacked.append(jnp.concatenate(pieces, axis=1))
    squares = jnp.concatenate(stacked, axis=0)
    out_ref[...] = jnp.dot(
        match_ref[...], squares, preferred_element_type=jnp.float32
    ).astype(jnp.bfloat16)


def select_kernel(target_ref, out_ref):
    hit = lax.broadcasted_iota(jnp.int32, out_ref.shape, 0) == target_ref[...]
    out_ref[...] = jnp.where(hit, 1.0, 0.0).astype(jnp.bfloat16)


def merge_kernel(me_ref, select_ref, arrived_ref, tables_ref, out_ref, numer_ref, denom_ref):
    step = pl.program_id(0)
    rows = out_ref.shape[0]
    cols = arrived_ref.shape[1]

    @pl.when(step == 0)
    def _():
        numer_ref[...] = jnp.zeros_like(numer_ref)
        denom_ref[...] = jnp.zeros_like(denom_ref)

    fisher = jnp.dot(select_ref[...], arrived_ref[...], preferred_element_type=jnp.float32)
    for b in range(SUB):
        at = slice(b * cols, (b + 1) * cols)
        weight = (fisher[b * rows : (b + 1) * rows] + prior_weight).astype(jnp.bfloat16)
        weight = weight.astype(jnp.float32)
        term = (weight * tables_ref[0, :, at].astype(jnp.float32)).astype(jnp.bfloat16)
        numer_ref[:, at] += term.astype(jnp.float32)
        denom_ref[:, at] += weight

    @pl.when(step == pl.num_programs(0) - 1)
    def _():
        out_ref[...] = (numer_ref[...] / denom_ref[...]).astype(jnp.bfloat16)


def per_device(token_ids, grad_values, grad_scales, tables):
    groups = lax.axis_size("vocab")
    ckpts = lax.axis_size("ckpt")
    me = lax.axis_index("ckpt")
    rows = tables.shape[1]
    width = tables.shape[2]
    count = token_ids.shape[0]
    quarter = width // ckpts
    cols = quarter // SUB

    owner = token_ids // rows
    same = owner[:, None] == owner[None, :]
    before = lax.broadcasted_iota(jnp.int32, (count, count), 0) < lax.broadcasted_iota(
        jnp.int32, (count, count), 1
    )
    rank = jnp.sum((same & before).astype(jnp.int32), axis=0)
    slot = owner * CAP + rank
    match = lax.broadcasted_iota(jnp.int32, (groups * CAP, count), 0) == slot[None, :]
    row_tags = (
        jnp.sum(jnp.where(match, (token_ids % rows)[None, :], 0), axis=1)
        .astype(jnp.bfloat16)
        .reshape(groups, CAP)
    )
    arrived_rows = lax.all_to_all(row_tags, "vocab", split_axis=0, concat_axis=0, tiled=True)

    chunk = CAP * SUB
    buffer = pl.pallas_call(
        place_kernel,
        grid=(ckpts,),
        in_specs=[
            pl.BlockSpec((1, count), lambda i: (0, 0)),
            pl.BlockSpec((quarter // BLK, count), lambda i: (i, 0)),
            pl.BlockSpec((count, quarter), lambda i: (0, i)),
        ],
        out_specs=pl.BlockSpec((groups * chunk, cols), lambda i: (i, 0)),
        out_shape=jax.ShapeDtypeStruct((ckpts * groups * chunk, cols), jnp.bfloat16),
        scratch_shapes=[pltpu.VMEM((groups * chunk, SUB * count), jnp.bfloat16)],
        compiler_params=pltpu.CompilerParams(vmem_limit_bytes=56 << 20),
        name="place",
    )(slot[None, :], grad_scales[0], grad_values[0])

    arrived = lax.all_to_all(
        buffer.reshape(ckpts * groups, chunk, cols),
        ("ckpt", "vocab"),
        split_axis=0,
        concat_axis=0,
        tiled=True,
    ).reshape(ckpts * groups * chunk, cols)

    def part(k):
        at = lax.rem(me + k, ckpts) * quarter
        return lax.dynamic_slice(tables[0], (0, at), (rows, quarter))

    held = [part(0)]
    for k in range(1, ckpts):
        held.append(lax.ppermute(part(k), "ckpt", [(i, (i + k) % ckpts) for i in range(ckpts)]))
    held = jnp.stack(held)

    target = arrived_rows.astype(jnp.int32).reshape(groups * CAP, 1) + rows * jnp.arange(
        SUB, dtype=jnp.int32
    )
    select = pl.pallas_call(
        select_kernel,
        out_shape=jax.ShapeDtypeStruct((SUB * rows, groups * chunk), jnp.bfloat16),
        compiler_params=pltpu.CompilerParams(vmem_limit_bytes=16 << 20),
        name="select",
    )(target.reshape(1, groups * chunk))

    return pl.pallas_call(
        merge_kernel,
        grid_spec=pltpu.PrefetchScalarGridSpec(
            num_scalar_prefetch=1,
            grid=(ckpts,),
            in_specs=[
                pl.BlockSpec((SUB * rows, groups * chunk), lambda k, me: (0, 0)),
                pl.BlockSpec(
                    (groups * chunk, cols), lambda k, me: (lax.rem(me[0] - k + ckpts, ckpts), 0)
                ),
                pl.BlockSpec((1, rows, quarter), lambda k, me: (k, 0, 0)),
            ],
            out_specs=pl.BlockSpec((rows, quarter), lambda k, me: (0, 0)),
            scratch_shapes=[
                pltpu.VMEM((rows, quarter), jnp.float32),
                pltpu.VMEM((rows, quarter), jnp.float32),
            ],
        ),
        out_shape=jax.ShapeDtypeStruct((rows, quarter), jnp.bfloat16),
        compiler_params=pltpu.CompilerParams(vmem_limit_bytes=32 << 20),
        name="merge",
    )(me.astype(jnp.int32)[None], select, arrived, held)


def solution(mesh):
    return jax.shard_map(
        per_device,
        mesh=mesh,
        in_specs=(
            P("vocab"),
            P("ckpt", "vocab", None),
            P("ckpt", None, "vocab"),
            P("ckpt", "vocab", None),
        ),
        out_specs=P("vocab", "ckpt"),
        check_vma=False,
    )
```

time: 251 us -> 150 us (0.60)
  waiting for transfers between devices: 172 us -> 87.2 us
  local copies, waits for them, and re-layouts: 17.8 us -> 2.24 us
  Pallas kernels: 0 us -> 13.4 us
  between operations: 13.5 us -> 0.13 us
  starting transfers between devices: 32.7 us -> 43.1 us
  matrix products: 10.2 us -> 0 us
    reduce_scatter x2 -> x0, waiting for transfers between devices: 75.5 us -> none  [the longest x1 37.9 us: per_device(): lax.psum_scatter(weight, 'ckpt', scatter_dimension=1, tiled=True)]
    all_to_all x1, waiting for transfers between devices: 96.1 us -> 39 us  [per_device(): lax.all_to_all(buffer.reshape(ckpts * groups, chunk, cols), ('ckpt', 'voc...]
    ppermute x0 -> x3, waiting for transfers between devices: none -> 43.8 us  [per_device(): lax.ppermute(part(k), 'ckpt', [(i, (i + k) % ckpts) for i in range(ckpts)])]
    reshape x2 -> x0, local copies, waits for them, and re-layouts: 14.8 us -> none  [the longest x1 7.62 us: per_device(): buffer = placed.astype(jnp.bfloat16).reshape(groups, capacity, width)]
    pallas_call x0 -> x3, Pallas kernels: none -> 13.4 us  [the longest x1 7.04 us: per_device(): pl.pallas_call(place_kernel, grid=(ckpts,), in_specs=[pl.BlockSpec((1, co...]
    dot_general x2 -> x0, matrix products: 10.2 us -> none  [the longest x1 5.11 us: per_device(): jnp.dot(selector, arrived.reshape(groups * capacity, width), preferred_el...]
    ppermute x0 -> x3, starting transfers between devices: none -> 9.47 us  [per_device(): lax.ppermute(part(k), 'ckpt', [(i, (i + k) % ckpts) for i in range(ckpts)])]
    all_to_all x1, waiting for transfers between devices: 0.01 us -> 4.33 us  [per_device(): lax.all_to_all(row_tags, 'vocab', split_axis=0, concat_axis=0, tiled=True)]
  transfers between devices with their start and end apart: 4 -> 5, of which waited for: 3 -> 5; matrix products, arithmetic and copies ran while one was open for 6% -> 2% of each run, Pallas kernels for 0% -> 5%
where the time goes in v1:
time: 150 us; the launch traced here: 149 us
  waiting for transfers between devices  87.2 us (58%)
  starting transfers between devices  43.1 us (29%)
  Pallas kernels  13.4 us (9%)
  other arithmetic  2.99 us (2%)
  local copies, waits for them, and re-layouts  2.24 us (1%)
    ppermute x3, waiting for transfers between devices, per_device(): lax.ppermute(part(k), 'ckpt', [(i, (i + k) % ckpts) for i in range(ckpts)])  43.8 us
    all_to_all x1, waiting for transfers between devices, per_device(): lax.all_to_all(buffer.reshape(ckpts * groups, chunk, cols), ('ckpt', 'voc...  39 us
    all_to_all x1, starting transfers between devices, per_device(): lax.all_to_all(row_tags, 'vocab', split_axis=0, concat_axis=0, tiled=True)  18.4 us
    all_to_all x1, starting transfers between devices, per_device(): lax.all_to_all(buffer.reshape(ckpts * groups, chunk, cols), ('ckpt', 'voc...  15.2 us
    ppermute x3, starting transfers between devices, per_device(): lax.ppermute(part(k), 'ckpt', [(i, (i + k) % ckpts) for i in range(ckpts)])  9.47 us
    pallas_call x1, Pallas kernels, per_device(): pl.pallas_call(place_kernel, grid=(ckpts,), in_specs=[pl.BlockSpec((1, co...  7.04 us
    pallas_call x1, Pallas kernels, per_device(): pl.pallas_call(merge_kernel, grid_spec=pltpu.PrefetchScalarGridSpec(num_s...  6.19 us
    all_to_all x1, waiting for transfers between devices, per_device(): lax.all_to_all(row_tags, 'vocab', split_axis=0, concat_axis=0, tiled=True)  4.33 us
  transfers between devices with their start and end apart: 5, of which 5 were waited for; matrix products, arithmetic and copies ran while one was open for 2% of the time, Pallas kernels for 5%

profile of v1, /device:TPU:1, one launch (start us, length us, event | category | flops | bytes accessed | tf_op | source)
XLA Modules:
  0.0 149.0 jit_solution(10574047919166163444)
XLA Ops:
  0.0 0.7 and_select_fusion.1
  0.7 0.1 convert_reduce_fusion.1
  0.8 0.0 copy-start.2
  0.8 0.1 select_reduce_fusion
  0.9 0.8 convert_element_type.33
  1.7 18.4 %all-to-all-start = ((bf16[128,1,2]{2,1,0:T(2,128)(2,1)}), bf16[128,1,2]{2,1,0:T(2,128)(2,1)S(1)}, u32[]{:S(2)}, u32[]{:S(2)}) async-start(bf16[128,1,2]{2,1,0:T(2,128)(2,1)} %convert_element_type.33), calls=%async_computation | async-start | bytes 131072 | tf_op jit(solution)/shard_map/all_to_all | solution.py:100
  20.1 0.0 copy-done.2
  20.2 7.0 %place.1 = bf16[4096,512]{1,0:T(8,128)(2,1)} custom-call(s32[1,128]{1,0:T(1,128)} %bitcast.19, f32[64,128]{1,0:T(8,128)} %bitcast.18, bf16[128,8192]{1,0:T(8,128)(2,1)} %bitcast.16), custom_call_target="tpu_custom_call" | custom-call | tf_op jit(solution)/shard_map/place/pallas_call | solution.py:103
  27.2 4.3 %all-to-all-done = bf16[128,1,2]{2,1,0:T(2,128)(2,1)S(1)} async-done(((bf16[128,1,2]{2,1,0:T(2,128)(2,1)}), bf16[128,1,2]{2,1,0:T(2,128)(2,1)S(1)}, u32[]{:S(2)}, u32[]{:S(2)}) %all-to-all-start) | async-done | bytes 544 | tf_op jit(solution)/shard_map/all_to_all | solution.py:100
  31.5 0.0 copy-start
  31.5 15.2 %all-to-all-start.1 = ((bf16[512,8,512]{2,1,0:T(8,128)(2,1)}), bf16[512,8,512]{2,1,0:T(8,128)(2,1)}, u32[]{:S(2)}, u32[]{:S(2)}) async-start(bf16[512,8,512]{2,1,0:T(8,128)(2,1)} %bitcast.15), calls=%async_computation.1 | async-start | bytes 8388608 | tf_op jit(solution)/shard_map/all_to_all | solution.py:118
  46.8 0.0 copy-done
  46.8 1.2 constant_dynamic-slice_fusion
  47.9 4.5 %collective-permute-start.2 = (bf16[128,2048]{1,0:T(8,128)(2,1)}, bf16[128,2048]{1,0:T(8,128)(2,1)S(1)}, u32[]{:S(2)}, u32[]{:S(2)}) collective-permute-start(bf16[128,2048]{1,0:T(8,128)(2,1)} %get-tuple-element.7), channel_id=1, source_target_pairs={{0,384},{128,0},{256,128},{384,256},{1,385},{129,1},{257,129},{385... | collective-permute-start | bytes 1572872 | tf_op jit(solution)/shard_map/ppermute | solution.py:132
  52.4 2.5 %collective-permute-start.1 = (bf16[128,2048]{1,0:T(8,128)(2,1)S(1)}, bf16[128,2048]{1,0:T(8,128)(2,1)}, u32[]{:S(2)}, u32[]{:S(2)}) collective-permute-start(bf16[128,2048]{1,0:T(8,128)(2,1)S(1)} %get-tuple-element.8), channel_id=1, source_target_pairs={{0,256},{128,384},{256,0},{384,128},{1,257},{129,385},{257,1},{385... | collective-permute-start | bytes 1572872 | tf_op jit(solution)/shard_map/ppermute | solution.py:132
  54.9 2.5 %collective-permute-start = (bf16[128,2048]{1,0:T(8,128)(2,1)S(1)}, bf16[128,2048]{1,0:T(8,128)(2,1)}, u32[]{:S(2)}, u32[]{:S(2)}) collective-permute-start(bf16[128,2048]{1,0:T(8,128)(2,1)S(1)} %get-tuple-element.6), channel_id=1, source_target_pairs={{0,128},{128,256},{256,384},{384,0},{1,129},{129,257},{257,385},{3... | collective-permute-start | bytes 1572872 | tf_op jit(solution)/shard_map/ppermute | solution.py:132
  57.4 0.2 convert_reduce_fusion
  57.7 0.1 reshape.67
  57.8 0.1 broadcast_add_fusion
  57.9 0.1 add.59.target_ref
  58.0 0.2 select.15.select_ref
  58.2 16.3 %collective-permute-done.2 = bf16[128,2048]{1,0:T(8,128)(2,1)S(1)} collective-permute-done((bf16[128,2048]{1,0:T(8,128)(2,1)}, bf16[128,2048]{1,0:T(8,128)(2,1)S(1)}, u32[]{:S(2)}, u32[]{:S(2)}) %collective-permute-start.2) | collective-permute-done | bytes 524320 | tf_op jit(solution)/shard_map/ppermute | solution.py:132
  74.5 0.0 copy-start.1
  74.5 3.4 %collective-permute-done.1 = bf16[128,2048]{1,0:T(8,128)(2,1)} collective-permute-done((bf16[128,2048]{1,0:T(8,128)(2,1)S(1)}, bf16[128,2048]{1,0:T(8,128)(2,1)}, u32[]{:S(2)}, u32[]{:S(2)}) %collective-permute-start.1) | collective-permute-done | bytes 524320 | tf_op jit(solution)/shard_map/ppermute | solution.py:132
  77.9 24.2 %collective-permute-done = bf16[128,2048]{1,0:T(8,128)(2,1)} collective-permute-done((bf16[128,2048]{1,0:T(8,128)(2,1)S(1)}, bf16[128,2048]{1,0:T(8,128)(2,1)}, u32[]{:S(2)}, u32[]{:S(2)}) %collective-permute-start) | collective-permute-done | bytes 524320 | tf_op jit(solution)/shard_map/ppermute | solution.py:132
  102.0 0.0 copy-done.1
  102.0 1.8 %pad_maximum_fusion.tables_ref = bf16[4,128,2048]{2,1,0:T(8,128)(2,1)S(1)} fusion(bf16[1,128,2048]{2,1,0:T(8,128)(2,1)} %bitcast.17, bf16[1,128,2048]{2,1,0:T(8,128)(2,1)} %bitcast.9, bf16[1,128,2048]{2,1,0:T(8,128)(2,1)} %bitcast.7, bf16[1,128,2048]{2,1,0:T(8,128)(2,1)} %get-tuple-element.5), kind=kLoop, calls=%fused_computation | loop fusion | flops 3145728 | bytes 4194304 | tf_op jit(solution)/shard_map/stack | solution.py:133
  103.8 39.0 %all-to-all-done.1 = bf16[512,8,512]{2,1,0:T(8,128)(2,1)} async-done(((bf16[512,8,512]{2,1,0:T(8,128)(2,1)}), bf16[512,8,512]{2,1,0:T(8,128)(2,1)}, u32[]{:S(2)}, u32[]{:S(2)}) %all-to-all-start.1) | async-done | bytes 4194336 | tf_op jit(solution)/shard_map/all_to_all | solution.py:118
  142.8 6.2 %merge.1 = bf16[128,2048]{1,0:T(8,128)(2,1)} custom-call(s32[1]{0:T(128)} %bitcast.me_ref, bf16[512,1024]{1,0:T(8,128)(2,1)S(1)} %select.15.select_ref, bf16[4096,512]{1,0:T(8,128)(2,1)} %bitcast.5.arrived_ref, bf16[4,128,2048]{2,1,0:T(8,128)(2,1)S(1)} %pad_maximum_fusion.tables_ref), custom_call_target="tpu_custom_call" | custom-call | tf_op jit(solution)/shard_map/merge/pallas_call | solution.py:145
  (3 shorter events, 0.0 us)
Async XLA Ops:
  0.8 19.4 %copy-start.2 = (s32[128]{0:T(128)}, s32[128]{0:T(128)S(1)}, u32[]{:S(2)}) copy-start(s32[128]{0:T(128)S(1)} %multiply_add_fusion) | copy-start | bytes 1540
  1.7 29.8 %all-to-all-start = ((bf16[128,1,2]{2,1,0:T(2,128)(2,1)}), bf16[128,1,2]{2,1,0:T(2,128)(2,1)S(1)}, u32[]{:S(2)}, u32[]{:S(2)}) async-start(bf16[128,1,2]{2,1,0:T(2,128)(2,1)} %convert_element_type.33), calls=%async_computation | async-start | bytes 131072 | tf_op jit(solution)/shard_map/all_to_all | solution.py:100
  31.5 15.3 %copy-start = (bf16[1,128,8192]{2,1,0:T(8,128)(2,1)S(1)}, bf16[1,128,8192]{2,1,0:T(8,128)(2,1)}, u32[]{:S(2)}) copy-start(bf16[1,128,8192]{2,1,0:T(8,128)(2,1)} %param.7) | copy-start | bytes 6291460
  31.5 111.3 %all-to-all-start.1 = ((bf16[512,8,512]{2,1,0:T(8,128)(2,1)}), bf16[512,8,512]{2,1,0:T(8,128)(2,1)}, u32[]{:S(2)}, u32[]{:S(2)}) async-start(bf16[512,8,512]{2,1,0:T(8,128)(2,1)} %bitcast.15), calls=%async_computation.1 | async-start | bytes 8388608 | tf_op jit(solution)/shard_map/all_to_all | solution.py:118
  47.9 26.5 %collective-permute-start.2 = (bf16[128,2048]{1,0:T(8,128)(2,1)}, bf16[128,2048]{1,0:T(8,128)(2,1)S(1)}, u32[]{:S(2)}, u32[]{:S(2)}) collective-permute-start(bf16[128,2048]{1,0:T(8,128)(2,1)} %get-tuple-element.7), channel_id=1, source_target_pairs={{0,384},{128,0},{256,128},{384,256},{1,385},{129,1},{257,129},{385... | collective-permute-start | bytes 1572872 | tf_op jit(solution)/shard_map/ppermute | solution.py:132
  52.4 25.4 %collective-permute-start.1 = (bf16[128,2048]{1,0:T(8,128)(2,1)S(1)}, bf16[128,2048]{1,0:T(8,128)(2,1)}, u32[]{:S(2)}, u32[]{:S(2)}) collective-permute-start(bf16[128,2048]{1,0:T(8,128)(2,1)S(1)} %get-tuple-element.8), channel_id=1, source_target_pairs={{0,256},{128,384},{256,0},{384,128},{1,257},{129,385},{257,1},{385... | collective-permute-start | bytes 1572872 | tf_op jit(solution)/shard_map/ppermute | solution.py:132
  54.9 47.1 %collective-permute-start = (bf16[128,2048]{1,0:T(8,128)(2,1)S(1)}, bf16[128,2048]{1,0:T(8,128)(2,1)}, u32[]{:S(2)}, u32[]{:S(2)}) collective-permute-start(bf16[128,2048]{1,0:T(8,128)(2,1)S(1)} %get-tuple-element.6), channel_id=1, source_target_pairs={{0,128},{128,256},{256,384},{384,0},{1,129},{129,257},{257,385},{3... | collective-permute-start | bytes 1572872 | tf_op jit(solution)/shard_map/ppermute | solution.py:132
  74.5 27.5 %copy-start.1 = (bf16[128,2048]{1,0:T(8,128)(2,1)}, bf16[128,2048]{1,0:T(8,128)(2,1)S(1)}, u32[]{:S(2)}) copy-start(bf16[128,2048]{1,0:T(8,128)(2,1)S(1)} %collective-permute-done.2) | copy-start | bytes 1572868

commit v2 on v1

v2 whole, which is shorter than its diff:
```python
import functools

import jax
import jax.numpy as jnp
from jax import lax
from jax.experimental import pallas as pl
from jax.experimental.pallas import tpu as pltpu
from jax.sharding import PartitionSpec as P

BLK = 128
CAP = 2
SUB = 4
NEAR = 32

prior_weight = 1.0


def place_kernel(slot_ref, scales_ref, grads_hbm, out_hbm, grads, placed, match, squares, in_sems, out_sems):
    parts, count, quarter = grads.shape
    rows = match.shape[0]
    cols = quarter // SUB
    copies_in = []
    for i in range(parts):
        copy = pltpu.make_async_copy(
            grads_hbm.at[:, i * quarter : (i + 1) * quarter], grads.at[i], in_sems.at[i]
        )
        copy.start()
        copies_in.append(copy)
    slot = slot_ref[...]
    for b in range(SUB):
        target = (slot // CAP) * (CAP * SUB) + (slot % CAP) * SUB + b
        hit = lax.broadcasted_iota(jnp.int32, (rows, count), 0) == target
        match[:, b * count : (b + 1) * count] = jnp.where(hit, 1.0, 0.0).astype(jnp.bfloat16)
    scales = scales_ref[...]
    blocks = scales.shape[0]
    scales = jnp.concatenate([scales, jnp.zeros((-blocks % BLK, count), jnp.float32)], axis=0).T
    per = cols // BLK
    copies_out = []
    for i in range(parts):
        copies_in[i].wait()
        for j in range(SUB * per):
            at = i * SUB * per + j
            scaled = grads[i, :, j * BLK : (j + 1) * BLK].astype(jnp.float32) * scales[:, at : at + 1]
            b, n = divmod(j, per)
            squares[i, b * count : (b + 1) * count, n * BLK : (n + 1) * BLK] = (
                scaled * scaled
            ).astype(jnp.bfloat16)
        here = slice(i * rows, (i + 1) * rows)
        placed[here, :] = jnp.dot(
            match[...], squares[i], preferred_element_type=jnp.float32
        ).astype(jnp.bfloat16)
        copy = pltpu.make_async_copy(placed.at[here], out_hbm.at[here], out_sems.at[i])
        copy.start()
        copies_out.append(copy)
    for copy in copies_out:
        copy.wait()


def select_kernel(target_ref, out_ref):
    hit = lax.broadcasted_iota(jnp.int32, out_ref.shape, 0) == target_ref[...]
    out_ref[...] = jnp.where(hit, 1.0, 0.0).astype(jnp.bfloat16)


def merge_kernel(me_ref, select_ref, arrived_hbm, tables_ref, out_ref, arrived, fisher, sems):
    parts, depth, cols = arrived.shape
    rows = out_ref.shape[0]
    copies = []
    for k in range(parts):
        at = pl.multiple_of(lax.rem(me_ref[0] + (parts - k), parts) * depth, depth)
        copy = pltpu.make_async_copy(arrived_hbm.at[pl.ds(at, depth)], arrived.at[k], sems.at[k])
        copy.start()
        copies.append(copy)
    for k in range(parts):
        copies[k].wait()
        fisher[k] = jnp.dot(select_ref[...], arrived[k], preferred_element_type=jnp.float32)
    for b in range(SUB):
        at = slice(b * cols, (b + 1) * cols)
        numer = denom = None
        for k in range(parts):
            weight = (fisher[k, b * rows : (b + 1) * rows] + prior_weight).astype(jnp.bfloat16)
            weight = weight.astype(jnp.float32)
            term = (weight * tables_ref[k, :, at].astype(jnp.float32)).astype(jnp.bfloat16)
            term = term.astype(jnp.float32)
            numer = term if numer is None else numer + term
            denom = weight if denom is None else denom + weight
        out_ref[:, at] = (numer / denom).astype(jnp.bfloat16)


def per_device(token_ids, grad_values, grad_scales, tables):
    groups = lax.axis_size("vocab")
    ckpts = lax.axis_size("ckpt")
    me = lax.axis_index("ckpt")
    rows = tables.shape[1]
    width = tables.shape[2]
    count = token_ids.shape[0]
    quarter = width // ckpts
    cols = quarter // SUB

    near = min(NEAR, groups)
    far = groups // near
    owner = lax.div(token_ids, rows)
    same = owner[:, None] == owner[None, :]
    before = lax.broadcasted_iota(jnp.int32, (count, count), 0) < lax.broadcasted_iota(
        jnp.int32, (count, count), 1
    )
    rank = jnp.sum((same & before).astype(jnp.int32), axis=0)
    slot = owner * CAP + rank
    tag_slot = (lax.rem(owner, near) * far + lax.div(owner, near)) * CAP + rank
    match = lax.broadcasted_iota(jnp.int32, (groups * CAP, count), 0) == tag_slot[None, :]
    row_tags = jnp.sum(jnp.where(match, lax.rem(token_ids, rows)[None, :], 0), axis=1)
    near_rows = lax.all_to_all(
        row_tags.reshape(near, far * CAP),
        "vocab",
        split_axis=0,
        concat_axis=0,
        axis_index_groups=[[f * near + n for n in range(near)] for f in range(far)],
        tiled=True,
    )

    chunk = CAP * SUB
    buffer = pl.pallas_call(
        place_kernel,
        in_specs=[
            pl.BlockSpec(memory_space=pltpu.VMEM),
            pl.BlockSpec(memory_space=pltpu.VMEM),
            pl.BlockSpec(memory_space=pltpu.HBM),
        ],
        out_specs=pl.BlockSpec(memory_space=pltpu.HBM),
        out_shape=jax.ShapeDtypeStruct((ckpts * groups * chunk, cols), jnp.bfloat16),
        scratch_shapes=[
            pltpu.VMEM((ckpts, count, quarter), jnp.bfloat16),
            pltpu.VMEM((ckpts * groups * chunk, cols), jnp.bfloat16),
            pltpu.VMEM((groups * chunk, SUB * count), jnp.bfloat16),
            pltpu.VMEM((ckpts, SUB * count, cols), jnp.bfloat16),
            pltpu.SemaphoreType.DMA((ckpts,)),
            pltpu.SemaphoreType.DMA((ckpts,)),
        ],
        compiler_params=pltpu.CompilerParams(vmem_limit_bytes=56 << 20),
        name="place",
    )(slot[None, :], grad_scales[0], grad_values[0])

    arrived = lax.all_to_all(
        buffer.reshape(ckpts * groups, chunk, cols),
        ("ckpt", "vocab"),
        split_axis=0,
        concat_axis=0,
        tiled=True,
    ).reshape(ckpts * groups * chunk, cols)

    def part(k):
        at = lax.rem(me + k, ckpts) * quarter
        return lax.dynamic_slice(tables[0], (0, at), (rows, quarter))

    held = [part(0)]
    for k in (1, 2, 3):
        piece = part(k)
        if k == 3:
            piece, held[1] = lax.optimization_barrier((piece, held[1]))
        held.append(lax.ppermute(piece, "ckpt", [(i, (i + k) % ckpts) for i in range(ckpts)]))
    held = jnp.stack(held)

    far_me = lax.div(lax.axis_index("vocab"), near)
    near_rows = near_rows.reshape(near, far, CAP)
    passed = []
    for m in range(far):
        piece = lax.dynamic_slice(
            near_rows, (0, lax.rem(far_me + (far - m), far), 0), (near, 1, CAP)
        ).reshape(1, near * CAP)
        if m:
            piece = lax.ppermute(
                piece, "vocab", [(v, (v + groups - m * near) % groups) for v in range(groups)]
            )
        passed.append(piece)
    passed = jnp.concatenate(passed + passed, axis=0)
    arrived_rows = lax.dynamic_slice(
        passed, (lax.rem(far - far_me, far), 0), (far, near * CAP)
    ).reshape(groups * CAP, 1)
    target = arrived_rows + rows * jnp.arange(SUB, dtype=jnp.int32)
    select = pl.pallas_call(
        select_kernel,
        out_shape=jax.ShapeDtypeStruct((SUB * rows, groups * chunk), jnp.bfloat16),
        compiler_params=pltpu.CompilerParams(vmem_limit_bytes=16 << 20),
        name="select",
    )(target.reshape(1, groups * chunk))

    return pl.pallas_call(
        merge_kernel,
        in_specs=[
            pl.BlockSpec(memory_space=pltpu.SMEM),
            pl.BlockSpec(memory_space=pltpu.VMEM),
            pl.BlockSpec(memory_space=pltpu.HBM),
            pl.BlockSpec(memory_space=pltpu.VMEM),
        ],
        out_specs=pl.BlockSpec(memory_space=pltpu.VMEM),
        out_shape=jax.ShapeDtypeStruct((rows, quarter), jnp.bfloat16),
        scratch_shapes=[
            pltpu.VMEM((ckpts, groups * chunk, cols), jnp.bfloat16),
            pltpu.VMEM((ckpts, SUB * rows, cols), jnp.float32),
            pltpu.SemaphoreType.DMA((ckpts,)),
        ],
        compiler_params=pltpu.CompilerParams(vmem_limit_bytes=32 << 20),
        name="merge",
    )(me.astype(jnp.int32)[None], select, arrived, held)


def solution(mesh):
    return jax.shard_map(
        per_device,
        mesh=mesh,
        in_specs=(
            P("vocab"),
            P("ckpt", "vocab", None),
            P("ckpt", None, "vocab"),
            P("ckpt", "vocab", None),
        ),
        out_specs=P("vocab", "ckpt"),
        check_vma=False,
    )
```

time: 150 us -> 144 us (0.960)
  waiting for transfers between devices: 87.2 us -> 62.2 us
  starting transfers between devices: 43.1 us -> 61.9 us
    ppermute x3 -> x6, starting transfers between devices: 9.47 us -> 29.9 us  [the longest x3 15.8 us: per_device(): lax.ppermute(piece, 'vocab', [(v, (v + groups - m * near) % groups) for v...]
    all_to_all x1, waiting for transfers between devices: 39 us -> 19.6 us  [per_device(): lax.all_to_all(buffer.reshape(ckpts * groups, chunk, cols), ('ckpt', 'voc...]
    all_to_all x1, starting transfers between devices: 18.4 us -> 10.6 us  [per_device(): lax.all_to_all(row_tags.reshape(near, far * CAP), 'vocab', split_axis=0,...]
    all_to_all x1, starting transfers between devices: 15.2 us -> 21.4 us  [per_device(): lax.all_to_all(buffer.reshape(ckpts * groups, chunk, cols), ('ckpt', 'voc...]
    all_to_all x1, waiting for transfers between devices: 4.33 us -> 0.59 us  [per_device(): lax.all_to_all(row_tags.reshape(near, far * CAP), 'vocab', split_axis=0,...]
    ppermute x3 -> x6, waiting for transfers between devices: 43.8 us -> 42 us  [the longest x3 24.1 us: per_device(): lax.ppermute(piece, 'vocab', [(v, (v + groups - m * near) % groups) for v...]
  transfers between devices with their start and end apart: 5 -> 8, of which waited for: 5 -> 5; matrix products, arithmetic and copies ran while one was open for 2% -> 3% of each run, Pallas kernels for 5% -> 5%
where the time goes in v2:
time: 144 us
  waiting for transfers between devices  62.2 us (43%)
  starting transfers between devices  61.9 us (43%)
  Pallas kernels  13.1 us (9%)
  other arithmetic  3.34 us (2%)
  local copies, waits for them, and re-layouts  3.02 us (2%)
    ppermute x3, waiting for transfers between devices, per_device(): lax.ppermute(piece, 'vocab', [(v, (v + groups - m * near) % groups) for v...  24.1 us
    all_to_all x1, starting transfers between devices, per_device(): lax.all_to_all(buffer.reshape(ckpts * groups, chunk, cols), ('ckpt', 'voc...  21.4 us
    all_to_all x1, waiting for transfers between devices, per_device(): lax.all_to_all(buffer.reshape(ckpts * groups, chunk, cols), ('ckpt', 'voc...  19.6 us
    ppermute x3, waiting for transfers between devices, per_device(): lax.ppermute(piece, 'ckpt', [(i, (i + k) % ckpts) for i in range(ckpts)])  17.9 us
    ppermute x3, starting transfers between devices, per_device(): lax.ppermute(piece, 'vocab', [(v, (v + groups - m * near) % groups) for v...  15.8 us
    ppermute x3, starting transfers between devices, per_device(): lax.ppermute(piece, 'ckpt', [(i, (i + k) % ckpts) for i in range(ckpts)])  14.1 us
    all_to_all x1, starting transfers between devices, per_device(): lax.all_to_all(row_tags.reshape(near, far * CAP), 'vocab', split_axis=0,...  10.6 us
    pallas_call x1, Pallas kernels, per_device(): pl.pallas_call(place_kernel, in_specs=[pl.BlockSpec(memory_space=pltpu.VM...  7.17 us
  transfers between devices with their start and end apart: 8, of which 5 were waited for; matrix products, arithmetic and copies ran while one was open for 3% of the time, Pallas kernels for 5%

profile of v2, /device:TPU:1, one launch (start us, length us, event | category | flops | bytes accessed | tf_op | source)
XLA Modules:
  0.0 143.8 jit_solution(3979161773123562605)
XLA Ops:
  0.0 0.7 compare_select_fusion.4
  0.7 0.1 convert_reduce_fusion
  0.8 0.6 add_bitcast_fusion
  1.3 0.1 select_reduce_fusion
  1.5 0.7 all_to_all.9
  2.2 10.6 %all-to-all-start = ((s32[32,1,8]{2,1,0:T(1,128)}), s32[32,1,8]{2,1,0:T(1,128)S(1)}, u32[]{:S(2)}, u32[]{:S(2)}) async-start(s32[32,1,8]{2,1,0:T(1,128)} %bitcast.1), calls=%async_computation | async-start | bytes 32768 | tf_op jit(solution)/shard_map/all_to_all | solution.py:111
  12.7 7.2 %place.1 = bf16[4096,512]{1,0:T(8,128)(2,1)} custom-call(s32[1,128]{1,0:T(1,128)} %get-tuple-element.17.slot_ref, f32[64,128]{1,0:T(8,128)} %bitcast.29, bf16[128,8192]{1,0:T(8,128)(2,1)} %bitcast.27), custom_call_target="tpu_custom_call" | custom-call | tf_op jit(solution)/shard_map/place/pallas_call | solution.py:121
  19.9 0.6 all-to-all-done
  20.5 0.0 copy-start
  20.5 21.4 %all-to-all-start.1 = ((bf16[512,8,512]{2,1,0:T(8,128)(2,1)}), bf16[512,8,512]{2,1,0:T(8,128)(2,1)}, u32[]{:S(2)}, u32[]{:S(2)}) async-start(bf16[512,8,512]{2,1,0:T(8,128)(2,1)} %bitcast.26), calls=%async_computation.1 | async-start | bytes 8388608 | tf_op jit(solution)/shard_map/all_to_all | solution.py:142
  42.0 0.0 copy-done
  42.0 1.2 constant_dynamic-slice_fusion
  43.2 3.3 %collective-permute-start.3 = (bf16[128,2048]{1,0:T(8,128)(2,1)}, bf16[128,2048]{1,0:T(8,128)(2,1)S(1)}, u32[]{:S(2)}, u32[]{:S(2)}) collective-permute-start(bf16[128,2048]{1,0:T(8,128)(2,1)} %get-tuple-element.12), channel_id=1, source_target_pairs={{0,128},{128,256},{256,384},{384,0},{1,129},{129,257},{257,385},{3... | collective-permute-start | bytes 1572872 | tf_op jit(solution)/shard_map/ppermute | solution.py:159
  46.5 4.3 %collective-permute-start.4 = (bf16[128,2048]{1,0:T(8,128)(2,1)S(1)}, bf16[128,2048]{1,0:T(8,128)(2,1)}, u32[]{:S(2)}, u32[]{:S(2)}) collective-permute-start(bf16[128,2048]{1,0:T(8,128)(2,1)S(1)} %get-tuple-element.11), channel_id=1, source_target_pairs={{0,256},{128,384},{256,0},{384,128},{1,257},{129,385},{257,1},{385... | collective-permute-start | bytes 1572872 | tf_op jit(solution)/shard_map/ppermute | solution.py:159
  50.9 17.8 %collective-permute-done.3 = bf16[128,2048]{1,0:T(8,128)(2,1)S(1)} collective-permute-done((bf16[128,2048]{1,0:T(8,128)(2,1)}, bf16[128,2048]{1,0:T(8,128)(2,1)S(1)}, u32[]{:S(2)}, u32[]{:S(2)}) %collective-permute-start.3) | collective-permute-done | bytes 524320 | tf_op jit(solution)/shard_map/ppermute | solution.py:159
  68.7 0.0 copy-start.1
  68.7 6.6 %collective-permute-start.5 = (bf16[128,2048]{1,0:T(8,128)(2,1)S(1)}, bf16[128,2048]{1,0:T(8,128)(2,1)}, u32[]{:S(2)}, u32[]{:S(2)}) collective-permute-start(bf16[128,2048]{1,0:T(8,128)(2,1)S(1)} %get-tuple-element.8), channel_id=1, source_target_pairs={{0,384},{128,0},{256,128},{384,256},{1,385},{129,1},{257,129},{385... | collective-permute-start | bytes 1572872 | tf_op jit(solution)/shard_map/ppermute | solution.py:159
  75.3 0.1 copy.17
  75.4 0.1 copy.19
  75.5 0.1 reshape.66
  75.6 5.9 %collective-permute-start = (s32[1,64]{1,0:T(1,128)S(1)}, s32[1,64]{1,0:T(1,128)S(1)}, u32[]{:S(2)}, u32[]{:S(2)}) collective-permute-start(s32[1,64]{1,0:T(1,128)S(1)} %reshape.66), channel_id=1, source_target_pairs={{0,96},{1,97},{2,98},{3,99},{4,100},{5,101},{6,102},{7,103},{8,104... | collective-permute-start | bytes 776 | tf_op jit(solution)/shard_map/ppermute | solution.py:170
  81.5 0.1 copy.20
  81.6 0.1 reshape.67
  81.7 5.8 %collective-permute-start.1 = (s32[1,64]{1,0:T(1,128)S(1)}, s32[1,64]{1,0:T(1,128)S(1)}, u32[]{:S(2)}, u32[]{:S(2)}) collective-permute-start(s32[1,64]{1,0:T(1,128)S(1)} %reshape.67), channel_id=1, source_target_pairs={{0,64},{1,65},{2,66},{3,67},{4,68},{5,69},{6,70},{7,71},{8,72},{9,... | collective-permute-start | bytes 776 | tf_op jit(solution)/shard_map/ppermute | solution.py:170
  87.5 0.1 copy.21
  87.6 0.1 reshape.68
  87.7 4.0 %collective-permute-start.2 = (s32[1,64]{1,0:T(1,128)S(1)}, s32[1,64]{1,0:T(1,128)S(1)}, u32[]{:S(2)}, u32[]{:S(2)}) collective-permute-start(s32[1,64]{1,0:T(1,128)S(1)} %reshape.68), channel_id=1, source_target_pairs={{0,32},{1,33},{2,34},{3,35},{4,36},{5,37},{6,38},{7,39},{8,40},{9,... | collective-permute-start | bytes 776 | tf_op jit(solution)/shard_map/ppermute | solution.py:170
  91.7 0.1 copy.18
  91.8 0.1 reshape.65
  91.9 14.4 %collective-permute-done = s32[1,64]{1,0:T(1,128)S(1)} collective-permute-done((s32[1,64]{1,0:T(1,128)S(1)}, s32[1,64]{1,0:T(1,128)S(1)}, u32[]{:S(2)}, u32[]{:S(2)}) %collective-permute-start) | collective-permute-done | bytes 288 | tf_op jit(solution)/shard_map/ppermute | solution.py:170
  106.3 9.7 %collective-permute-done.1 = s32[1,64]{1,0:T(1,128)S(1)} collective-permute-done((s32[1,64]{1,0:T(1,128)S(1)}, s32[1,64]{1,0:T(1,128)S(1)}, u32[]{:S(2)}, u32[]{:S(2)}) %collective-permute-start.1) | collective-permute-done | bytes 288 | tf_op jit(solution)/shard_map/ppermute | solution.py:170
  116.0 0.0 collective-permute-done.2
  116.1 0.1 add.93
  116.2 0.1 broadcast_add_fusion
  116.3 0.1 add.97.target_ref
  116.4 0.2 select.29.select_ref
  116.6 0.0 collective-permute-done.4
  116.6 0.0 collective-permute-done.5
  116.6 0.0 copy-done.1
  116.6 1.8 %pad_maximum_fusion.tables_ref = bf16[4,128,2048]{2,1,0:T(8,128)(2,1)S(1)} fusion(bf16[1,128,2048]{2,1,0:T(8,128)(2,1)} %bitcast.13, bf16[1,128,2048]{2,1,0:T(8,128)(2,1)} %bitcast.12, bf16[1,128,2048]{2,1,0:T(8,128)(2,1)} %bitcast.28, bf16[1,128,2048]{2,1,0:T(8,128)(2,1)} %get-tuple-element.9), kind=kLoop, calls=%fused_computation | loop fusion | flops 3145728 | bytes 4194304 | tf_op jit(solution)/shard_map/stack | solution.py:160
  118.4 19.6 %all-to-all-done.1 = bf16[512,8,512]{2,1,0:T(8,128)(2,1)} async-done(((bf16[512,8,512]{2,1,0:T(8,128)(2,1)}), bf16[512,8,512]{2,1,0:T(8,128)(2,1)}, u32[]{:S(2)}, u32[]{:S(2)}) %all-to-all-start.1) | async-done | bytes 4194336 | tf_op jit(solution)/shard_map/all_to_all | solution.py:142
  138.0 5.8 %merge.1 = bf16[128,2048]{1,0:T(8,128)(2,1)} custom-call(s32[1]{0:T(128)} %bitcast.me_ref, bf16[512,1024]{1,0:T(8,128)(2,1)S(1)} %select.29.select_ref, bf16[4096,512]{1,0:T(8,128)(2,1)} %bitcast.7.arrived_hbm, bf16[4,128,2048]{2,1,0:T(8,128)(2,1)S(1)} %pad_maximum_fusion.tables_ref), custom_call_target="tpu_custom_call" | custom-call | tf_op jit(solution)/shard_map/merge/pallas_call | solution.py:186
  (4 shorter events, 0.0 us)
Async XLA Ops:
  2.2 18.3 %all-to-all-start = ((s32[32,1,8]{2,1,0:T(1,128)}), s32[32,1,8]{2,1,0:T(1,128)S(1)}, u32[]{:S(2)}, u32[]{:S(2)}) async-start(s32[32,1,8]{2,1,0:T(1,128)} %bitcast.1), calls=%async_computation | async-start | bytes 32768 | tf_op jit(solution)/shard_map/all_to_all | solution.py:111
  20.5 21.5 %copy-start = (bf16[1,128,8192]{2,1,0:T(8,128)(2,1)S(1)}, bf16[1,128,8192]{2,1,0:T(8,128)(2,1)}, u32[]{:S(2)}) copy-start(bf16[1,128,8192]{2,1,0:T(8,128)(2,1)} %param.7) | copy-start | bytes 6291460
  20.5 117.5 %all-to-all-start.1 = ((bf16[512,8,512]{2,1,0:T(8,128)(2,1)}), bf16[512,8,512]{2,1,0:T(8,128)(2,1)}, u32[]{:S(2)}, u32[]{:S(2)}) async-start(bf16[512,8,512]{2,1,0:T(8,128)(2,1)} %bitcast.26), calls=%async_computation.1 | async-start | bytes 8388608 | tf_op jit(solution)/shard_map/all_to_all | solution.py:142
  43.2 25.5 %collective-permute-start.3 = (bf16[128,2048]{1,0:T(8,128)(2,1)}, bf16[128,2048]{1,0:T(8,128)(2,1)S(1)}, u32[]{:S(2)}, u32[]{:S(2)}) collective-permute-start(bf16[128,2048]{1,0:T(8,128)(2,1)} %get-tuple-element.12), channel_id=1, source_target_pairs={{0,128},{128,256},{256,384},{384,0},{1,129},{129,257},{257,385},{3... | collective-permute-start | bytes 1572872 | tf_op jit(solution)/shard_map/ppermute | solution.py:159
  46.5 70.1 %collective-permute-start.4 = (bf16[128,2048]{1,0:T(8,128)(2,1)S(1)}, bf16[128,2048]{1,0:T(8,128)(2,1)}, u32[]{:S(2)}, u32[]{:S(2)}) collective-permute-start(bf16[128,2048]{1,0:T(8,128)(2,1)S(1)} %get-tuple-element.11), channel_id=1, source_target_pairs={{0,256},{128,384},{256,0},{384,128},{1,257},{129,385},{257,1},{385... | collective-permute-start | bytes 1572872 | tf_op jit(solution)/shard_map/ppermute | solution.py:159
  68.7 47.9 %copy-start.1 = (bf16[128,2048]{1,0:T(8,128)(2,1)}, bf16[128,2048]{1,0:T(8,128)(2,1)S(1)}, u32[]{:S(2)}) copy-start(bf16[128,2048]{1,0:T(8,128)(2,1)S(1)} %collective-permute-done.3) | copy-start | bytes 1572868
  68.7 47.9 %collective-permute-start.5 = (bf16[128,2048]{1,0:T(8,128)(2,1)S(1)}, bf16[128,2048]{1,0:T(8,128)(2,1)}, u32[]{:S(2)}, u32[]{:S(2)}) collective-permute-start(bf16[128,2048]{1,0:T(8,128)(2,1)S(1)} %get-tuple-element.8), channel_id=1, source_target_pairs={{0,384},{128,0},{256,128},{384,256},{1,385},{129,1},{257,129},{385... | collective-permute-start | bytes 1572872 | tf_op jit(solution)/shard_map/ppermute | solution.py:159
  75.6 30.7 %collective-permute-start = (s32[1,64]{1,0:T(1,128)S(1)}, s32[1,64]{1,0:T(1,128)S(1)}, u32[]{:S(2)}, u32[]{:S(2)}) collective-permute-start(s32[1,64]{1,0:T(1,128)S(1)} %reshape.66), channel_id=1, source_target_pairs={{0,96},{1,97},{2,98},{3,99},{4,100},{5,101},{6,102},{7,103},{8,104... | collective-permute-start | bytes 776 | tf_op jit(solution)/shard_map/ppermute | solution.py:170
  81.7 34.4 %collective-permute-start.1 = (s32[1,64]{1,0:T(1,128)S(1)}, s32[1,64]{1,0:T(1,128)S(1)}, u32[]{:S(2)}, u32[]{:S(2)}) collective-permute-start(s32[1,64]{1,0:T(1,128)S(1)} %reshape.67), channel_id=1, source_target_pairs={{0,64},{1,65},{2,66},{3,67},{4,68},{5,69},{6,70},{7,71},{8,72},{9,... | collective-permute-start | bytes 776 | tf_op jit(solution)/shard_map/ppermute | solution.py:170
  87.7 28.3 %collective-permute-start.2 = (s32[1,64]{1,0:T(1,128)S(1)}, s32[1,64]{1,0:T(1,128)S(1)}, u32[]{:S(2)}, u32[]{:S(2)}) collective-permute-start(s32[1,64]{1,0:T(1,128)S(1)} %reshape.68), channel_id=1, source_target_pairs={{0,32},{1,33},{2,34},{3,35},{4,36},{5,37},{6,38},{7,39},{8,40},{9,... | collective-permute-start | bytes 776 | tf_op jit(solution)/shard_map/ppermute | solution.py:170

commit v3 on v2

--- a/solution.py
+++ b/solution.py
@@ -10,7 +10,7 @@
 BLK = 128
 CAP = 2
 SUB = 4
-NEAR = 32
+CORES = 2
 
 prior_weight = 1.0
 
@@ -36,8 +36,9 @@
     scales = jnp.concatenate([scales, jnp.zeros((-blocks % BLK, count), jnp.float32)], axis=0).T
     per = cols // BLK
     copies_out = []
+    for copy in copies_in:
+        copy.wait()
     for i in range(parts):
-        copies_in[i].wait()
         for j in range(SUB * per):
             at = i * SUB * per + j
             scaled = grads[i, :, j * BLK : (j + 1) * BLK].astype(jnp.float32) * scales[:, at : at + 1]
@@ -61,7 +62,7 @@
     out_ref[...] = jnp.where(hit, 1.0, 0.0).astype(jnp.bfloat16)
 
 
-def merge_kernel(me_ref, select_ref, arrived_hbm, tables_ref, out_ref, arrived, fisher, sems):
+def merge_kernel(me_ref, select_ref, arrived_hbm, tables_ref, out_ref, arrived, numer, denom, sems):
     parts, depth, cols = arrived.shape
     rows = out_ref.shape[0]
     copies = []
@@ -72,18 +73,21 @@
         copies.append(copy)
     for k in range(parts):
         copies[k].wait()
-        fisher[k] = jnp.dot(select_ref[...], arrived[k], preferred_element_type=jnp.float32)
-    for b in range(SUB):
-        at = slice(b * cols, (b + 1) * cols)
-        numer = denom = None
-        for k in range(parts):
-            weight = (fisher[k, b * rows : (b + 1) * rows] + prior_weight).astype(jnp.bfloat16)
+        fisher = jnp.dot(select_ref[...], arrived[k], preferred_element_type=jnp.float32)
+        for b in range(SUB):
+            at = slice(b * cols, (b + 1) * cols)
+            weight = (fisher[b * rows : (b + 1) * rows] + prior_weight).astype(jnp.bfloat16)
             weight = weight.astype(jnp.float32)
             term = (weight * tables_ref[k, :, at].astype(jnp.float32)).astype(jnp.bfloat16)
             term = term.astype(jnp.float32)
-            numer = term if numer is None else numer + term
-            denom = weight if denom is None else denom + weight
-        out_ref[:, at] = (numer / denom).astype(jnp.bfloat16)
+            if k == 0:
+                numer[:, at] = term
+                denom[:, at] = weight
+            elif k < parts - 1:
+                numer[:, at] += term
+                denom[:, at] += weight
+            else:
+                out_ref[:, at] = ((numer[:, at] + term) / (denom[:, at] + weight)).astype(jnp.bfloat16)
 
 
 def per_device(token_ids, grad_values, grad_scales, tables):
@@ -96,8 +100,7 @@
     quarter = width // ckpts
     cols = quarter // SUB
 
-    near = min(NEAR, groups)
-    far = groups // near
+    chips = groups // CORES
     owner = lax.div(token_ids, rows)
     same = owner[:, None] == owner[None, :]
     before = lax.broadcasted_iota(jnp.int32, (count, count), 0) < lax.broadcasted_iota(
@@ -105,15 +108,14 @@
     )
     rank = jnp.sum((same & before).astype(jnp.int32), axis=0)
     slot = owner * CAP + rank
-    tag_slot = (lax.rem(owner, near) * far + lax.div(owner, near)) * CAP + rank
-    match = lax.broadcasted_iota(jnp.int32, (groups * CAP, count), 0) == tag_slot[None, :]
+    match = lax.broadcasted_iota(jnp.int32, (groups * CAP, count), 0) == slot[None, :]
     row_tags = jnp.sum(jnp.where(match, lax.rem(token_ids, rows)[None, :], 0), axis=1)
-    near_rows = lax.all_to_all(
-        row_tags.reshape(near, far * CAP),
+    chip_rows = lax.all_to_all(
+        row_tags.reshape(chips, CORES * CAP),
         "vocab",
         split_axis=0,
         concat_axis=0,
-        axis_index_groups=[[f * near + n for n in range(near)] for f in range(far)],
+        axis_index_groups=[[n * CORES + core for n in range(chips)] for core in range(CORES)],
         tiled=True,
     )
 
@@ -152,29 +154,17 @@
         return lax.dynamic_slice(tables[0], (0, at), (rows, quarter))
 
     held = [part(0)]
-    for k in (1, 2, 3):
-        piece = part(k)
-        if k == 3:
-            piece, held[1] = lax.optimization_barrier((piece, held[1]))
-        held.append(lax.ppermute(piece, "ckpt", [(i, (i + k) % ckpts) for i in range(ckpts)]))
+    for k in range(1, ckpts):
+        held.append(lax.ppermute(part(k), "ckpt", [(i, (i + k) % ckpts) for i in range(ckpts)]))
     held = jnp.stack(held)
 
-    far_me = lax.div(lax.axis_index("vocab"), near)
-    near_rows = near_rows.reshape(near, far, CAP)
-    passed = []
-    for m in range(far):
-        piece = lax.dynamic_slice(
-            near_rows, (0, lax.rem(far_me + (far - m), far), 0), (near, 1, CAP)
-        ).reshape(1, near * CAP)
-        if m:
-            piece = lax.ppermute(
-                piece, "vocab", [(v, (v + groups - m * near) % groups) for v in range(groups)]
-            )
-        passed.append(piece)
-    passed = jnp.concatenate(passed + passed, axis=0)
-    arrived_rows = lax.dynamic_slice(
-        passed, (lax.rem(far - far_me, far), 0), (far, near * CAP)
-    ).reshape(groups * CAP, 1)
+    core = lax.rem(lax.axis_index("vocab"), CORES)
+    chip_rows = chip_rows.reshape(chips, CORES, CAP).transpose(1, 2, 0)
+    mine = lax.dynamic_slice(chip_rows, (core, 0, 0), (1, CAP, chips))[0]
+    other = lax.dynamic_slice(chip_rows, (CORES - 1 - core, 0, 0), (1, CAP, chips))[0]
+    other = lax.ppermute(other, "vocab", [(v, v ^ 1) for v in range(groups)])
+    even, odd = jnp.where(core == 0, mine, other), jnp.where(core == 0, other, mine)
+    arrived_rows = jnp.stack([even, odd]).transpose(2, 0, 1).reshape(groups * CAP, 1)
     target = arrived_rows + rows * jnp.arange(SUB, dtype=jnp.int32)
     select = pl.pallas_call(
         select_kernel,
@@ -195,7 +185,8 @@
         out_shape=jax.ShapeDtypeStruct((rows, quarter), jnp.bfloat16),
         scratch_shapes=[
             pltpu.VMEM((ckpts, groups * chunk, cols), jnp.bfloat16),
-            pltpu.VMEM((ckpts, SUB * rows, cols), jnp.float32),
+            pltpu.VMEM((rows, quarter), jnp.float32),
+            pltpu.VMEM((rows, quarter), jnp.float32),
             pltpu.SemaphoreType.DMA((ckpts,)),
         ],
         compiler_params=pltpu.CompilerParams(vmem_limit_bytes=32 << 20),

time: 144 us -> 147 us (1.021)
  waiting for transfers between devices: 62.2 us -> 82.8 us
  starting transfers between devices: 61.9 us -> 46.4 us
    all_to_all x1, waiting for transfers between devices: 19.6 us -> 39 us  [per_device(): lax.all_to_all(buffer.reshape(ckpts * groups, chunk, cols), ('ckpt', 'voc...]
    ppermute x6 -> x4, starting transfers between devices: 29.9 us -> 14 us  [the longest x3 9.47 us: per_device(): lax.ppermute(part(k), 'ckpt', [(i, (i + k) % ckpts) for i in range(ckpts)])]
    all_to_all x1, starting transfers between devices: 10.6 us -> 17.1 us  [per_device(): lax.all_to_all(row_tags.reshape(chips, CORES * CAP), 'vocab', split_axis=...]
    all_to_all x1, starting transfers between devices: 21.4 us -> 15.2 us  [per_device(): lax.all_to_all(buffer.reshape(ckpts * groups, chunk, cols), ('ckpt', 'voc...]
    all_to_all x1, waiting for transfers between devices: 0.59 us -> 4.6 us  [per_device(): lax.all_to_all(row_tags.reshape(chips, CORES * CAP), 'vocab', split_axis=...]
    ppermute x6 -> x4, waiting for transfers between devices: 42 us -> 39.2 us  [the longest x3 38.5 us: per_device(): lax.ppermute(part(k), 'ckpt', [(i, (i + k) % ckpts) for i in range(ckpts)])]
  transfers between devices with their start and end apart: 8 -> 6, of which waited for: 5 -> 6; matrix products, arithmetic and copies ran while one was open for 3% -> 2% of each run, Pallas kernels for 5% -> 4%
where the time goes in v3:
time: 147 us; the launch traced here: 146 us
  waiting for transfers between devices  82.8 us (56%)
  starting transfers between devices  46.4 us (32%)
  Pallas kernels  11.9 us (8%)
  other arithmetic  2.78 us (2%)
  local copies, waits for them, and re-layouts  2.39 us (2%)
    all_to_all x1, waiting for transfers between devices, per_device(): lax.all_to_all(buffer.reshape(ckpts * groups, chunk, cols), ('ckpt', 'voc...  39 us
    ppermute x3, waiting for transfers between devices, per_device(): lax.ppermute(part(k), 'ckpt', [(i, (i + k) % ckpts) for i in range(ckpts)])  38.5 us
    all_to_all x1, starting transfers between devices, per_device(): lax.all_to_all(row_tags.reshape(chips, CORES * CAP), 'vocab', split_axis=...  17.1 us
    all_to_all x1, starting transfers between devices, per_device(): lax.all_to_all(buffer.reshape(ckpts * groups, chunk, cols), ('ckpt', 'voc...  15.2 us
    ppermute x3, starting transfers between devices, per_device(): lax.ppermute(part(k), 'ckpt', [(i, (i + k) % ckpts) for i in range(ckpts)])  9.47 us
    pallas_call x1, Pallas kernels, per_device(): pl.pallas_call(place_kernel, in_specs=[pl.BlockSpec(memory_space=pltpu.VM...  6.15 us
    pallas_call x1, Pallas kernels, per_device(): pl.pallas_call(merge_kernel, in_specs=[pl.BlockSpec(memory_space=pltpu.SM...  5.52 us
    all_to_all x1, waiting for transfers between devices, per_device(): lax.all_to_all(row_tags.reshape(chips, CORES * CAP), 'vocab', split_axis=...  4.6 us
  transfers between devices with their start and end apart: 6, of which 6 were waited for; matrix products, arithmetic and copies ran while one was open for 2% of the time, Pallas kernels for 4%

profile of v3, /device:TPU:1, one launch (start us, length us, event | category | flops | bytes accessed | tf_op | source)
XLA Modules:
  0.0 146.4 jit_solution(17498893322674574489)
XLA Ops:
  0.0 0.7 compare_select_fusion.1
  0.7 0.1 convert_reduce_fusion
  0.8 0.0 copy-start.2
  0.8 0.1 select_reduce_fusion
  0.9 0.7 all_to_all.9
  1.6 17.1 %all-to-all-start = ((s32[64,1,4]{2,1,0:T(1,128)}), s32[64,1,4]{2,1,0:T(1,128)S(1)}, u32[]{:S(2)}, u32[]{:S(2)}) async-start(s32[64,1,4]{2,1,0:T(1,128)} %bitcast.1), calls=%async_computation | async-start | bytes 65536 | tf_op jit(solution)/shard_map/all_to_all | solution.py:113
  18.8 0.0 copy-done.2
  18.8 6.2 %place.1 = bf16[4096,512]{1,0:T(8,128)(2,1)} custom-call(s32[1,128]{1,0:T(1,128)} %bitcast.41, f32[64,128]{1,0:T(8,128)} %bitcast.38, bf16[128,8192]{1,0:T(8,128)(2,1)} %bitcast.36), custom_call_target="tpu_custom_call" | custom-call | tf_op jit(solution)/shard_map/place/pallas_call | solution.py:123
  24.9 4.6 %all-to-all-done = s32[64,1,4]{2,1,0:T(1,128)S(1)} async-done(((s32[64,1,4]{2,1,0:T(1,128)}), s32[64,1,4]{2,1,0:T(1,128)S(1)}, u32[]{:S(2)}, u32[]{:S(2)}) %all-to-all-start) | async-done | bytes 1056 | tf_op jit(solution)/shard_map/all_to_all | solution.py:113
  29.5 0.0 copy-start
  29.5 15.2 %all-to-all-start.1 = ((bf16[512,8,512]{2,1,0:T(8,128)(2,1)}), bf16[512,8,512]{2,1,0:T(8,128)(2,1)}, u32[]{:S(2)}, u32[]{:S(2)}) async-start(bf16[512,8,512]{2,1,0:T(8,128)(2,1)} %bitcast.35), calls=%async_computation.1 | async-start | bytes 8388608 | tf_op jit(solution)/shard_map/all_to_all | solution.py:144
  44.8 0.0 copy-done
  44.8 1.2 constant_dynamic-slice_fusion
  46.0 4.5 %collective-permute-start.3 = (bf16[128,2048]{1,0:T(8,128)(2,1)}, bf16[128,2048]{1,0:T(8,128)(2,1)S(1)}, u32[]{:S(2)}, u32[]{:S(2)}) collective-permute-start(bf16[128,2048]{1,0:T(8,128)(2,1)} %get-tuple-element.7), channel_id=1, source_target_pairs={{0,384},{128,0},{256,128},{384,256},{1,385},{129,1},{257,129},{385... | collective-permute-start | bytes 1572872 | tf_op jit(solution)/shard_map/ppermute | solution.py:158
  50.5 2.5 %collective-permute-start.2 = (bf16[128,2048]{1,0:T(8,128)(2,1)S(1)}, bf16[128,2048]{1,0:T(8,128)(2,1)}, u32[]{:S(2)}, u32[]{:S(2)}) collective-permute-start(bf16[128,2048]{1,0:T(8,128)(2,1)S(1)} %get-tuple-element.8), channel_id=1, source_target_pairs={{0,256},{128,384},{256,0},{384,128},{1,257},{129,385},{257,1},{385... | collective-permute-start | bytes 1572872 | tf_op jit(solution)/shard_map/ppermute | solution.py:158
  53.0 2.5 %collective-permute-start.1 = (bf16[128,2048]{1,0:T(8,128)(2,1)S(1)}, bf16[128,2048]{1,0:T(8,128)(2,1)}, u32[]{:S(2)}, u32[]{:S(2)}) collective-permute-start(bf16[128,2048]{1,0:T(8,128)(2,1)S(1)} %get-tuple-element.6), channel_id=1, source_target_pairs={{0,128},{128,256},{256,384},{384,0},{1,129},{129,257},{257,385},{3... | collective-permute-start | bytes 1572872 | tf_op jit(solution)/shard_map/ppermute | solution.py:158
  55.5 0.1 copy.14
  55.6 4.6 %collective-permute-start = (s32[2,64]{1,0:T(2,128)S(1)}, s32[2,64]{1,0:T(2,128)S(1)}, u32[]{:S(2)}, u32[]{:S(2)}) collective-permute-start(s32[2,64]{1,0:T(2,128)S(1)} %fusion.2), channel_id=1, source_target_pairs={{0,1},{1,0},{2,3},{3,2},{4,5},{5,4},{6,7},{7,6},{8,9},{9,8},{10,11... | collective-permute-start | bytes 1544 | tf_op jit(solution)/shard_map/ppermute | solution.py:165
  60.2 0.8 collective-permute-done
  60.9 0.1 copy.15
  61.1 0.2 add.59
  61.2 0.1 broadcast_add_fusion
  61.3 0.1 add.63.target_ref
  61.5 0.2 select.15.select_ref
  61.6 10.9 %collective-permute-done.3 = bf16[128,2048]{1,0:T(8,128)(2,1)S(1)} collective-permute-done((bf16[128,2048]{1,0:T(8,128)(2,1)}, bf16[128,2048]{1,0:T(8,128)(2,1)S(1)}, u32[]{:S(2)}, u32[]{:S(2)}) %collective-permute-start.3) | collective-permute-done | bytes 524320 | tf_op jit(solution)/shard_map/ppermute | solution.py:158
  72.5 0.0 copy-start.1
  72.5 3.4 %collective-permute-done.2 = bf16[128,2048]{1,0:T(8,128)(2,1)} collective-permute-done((bf16[128,2048]{1,0:T(8,128)(2,1)S(1)}, bf16[128,2048]{1,0:T(8,128)(2,1)}, u32[]{:S(2)}, u32[]{:S(2)}) %collective-permute-start.2) | collective-permute-done | bytes 524320 | tf_op jit(solution)/shard_map/ppermute | solution.py:158
  75.9 24.2 %collective-permute-done.1 = bf16[128,2048]{1,0:T(8,128)(2,1)} collective-permute-done((bf16[128,2048]{1,0:T(8,128)(2,1)S(1)}, bf16[128,2048]{1,0:T(8,128)(2,1)}, u32[]{:S(2)}, u32[]{:S(2)}) %collective-permute-start.1) | collective-permute-done | bytes 524320 | tf_op jit(solution)/shard_map/ppermute | solution.py:158
  100.1 0.0 copy-done.1
  100.1 1.8 %pad_maximum_fusion.tables_ref = bf16[4,128,2048]{2,1,0:T(8,128)(2,1)S(1)} fusion(bf16[1,128,2048]{2,1,0:T(8,128)(2,1)} %bitcast.37, bf16[1,128,2048]{2,1,0:T(8,128)(2,1)} %bitcast.19, bf16[1,128,2048]{2,1,0:T(8,128)(2,1)} %bitcast.17, bf16[1,128,2048]{2,1,0:T(8,128)(2,1)} %get-tuple-element.5), kind=kLoop, calls=%fused_computation | loop fusion | flops 3145728 | bytes 4194304 | tf_op jit(solution)/shard_map/stack | solution.py:159
  101.9 39.0 %all-to-all-done.1 = bf16[512,8,512]{2,1,0:T(8,128)(2,1)} async-done(((bf16[512,8,512]{2,1,0:T(8,128)(2,1)}), bf16[512,8,512]{2,1,0:T(8,128)(2,1)}, u32[]{:S(2)}, u32[]{:S(2)}) %all-to-all-start.1) | async-done | bytes 4194336 | tf_op jit(solution)/shard_map/all_to_all | solution.py:144
  140.9 5.5 %merge.1 = bf16[128,2048]{1,0:T(8,128)(2,1)} custom-call(s32[1]{0:T(128)} %bitcast.me_ref, bf16[512,1024]{1,0:T(8,128)(2,1)S(1)} %select.15.select_ref, bf16[4096,512]{1,0:T(8,128)(2,1)} %bitcast.15.arrived_hbm, bf16[4,128,2048]{2,1,0:T(8,128)(2,1)S(1)} %pad_maximum_fusion.tables_ref), custom_call_target="tpu_custom_call" | custom-call | tf_op jit(solution)/shard_map/merge/pallas_call | solution.py:176
  (5 shorter events, 0.0 us)
Async XLA Ops:
  0.8 18.0 %copy-start.2 = (s32[128]{0:T(128)}, s32[128]{0:T(128)S(1)}, u32[]{:S(2)}) copy-start(s32[128]{0:T(128)S(1)} %multiply_add_fusion) | copy-start | bytes 1540
  1.6 27.9 %all-to-all-start = ((s32[64,1,4]{2,1,0:T(1,128)}), s32[64,1,4]{2,1,0:T(1,128)S(1)}, u32[]{:S(2)}, u32[]{:S(2)}) async-start(s32[64,1,4]{2,1,0:T(1,128)} %bitcast.1), calls=%async_computation | async-start | bytes 65536 | tf_op jit(solution)/shard_map/all_to_all | solution.py:113
  29.5 15.3 %copy-start = (bf16[1,128,8192]{2,1,0:T(8,128)(2,1)S(1)}, bf16[1,128,8192]{2,1,0:T(8,128)(2,1)}, u32[]{:S(2)}) copy-start(bf16[1,128,8192]{2,1,0:T(8,128)(2,1)} %param.7) | copy-start | bytes 6291460
  29.5 111.3 %all-to-all-start.1 = ((bf16[512,8,512]{2,1,0:T(8,128)(2,1)}), bf16[512,8,512]{2,1,0:T(8,128)(2,1)}, u32[]{:S(2)}, u32[]{:S(2)}) async-start(bf16[512,8,512]{2,1,0:T(8,128)(2,1)} %bitcast.35), calls=%async_computation.1 | async-start | bytes 8388608 | tf_op jit(solution)/shard_map/all_to_all | solution.py:144
  46.0 26.6 %collective-permute-start.3 = (bf16[128,2048]{1,0:T(8,128)(2,1)}, bf16[128,2048]{1,0:T(8,128)(2,1)S(1)}, u32[]{:S(2)}, u32[]{:S(2)}) collective-permute-start(bf16[128,2048]{1,0:T(8,128)(2,1)} %get-tuple-element.7), channel_id=1, source_target_pairs={{0,384},{128,0},{256,128},{384,256},{1,385},{129,1},{257,129},{385... | collective-permute-start | bytes 1572872 | tf_op jit(solution)/shard_map/ppermute | solution.py:158
  50.5 25.4 %collective-permute-start.2 = (bf16[128,2048]{1,0:T(8,128)(2,1)S(1)}, bf16[128,2048]{1,0:T(8,128)(2,1)}, u32[]{:S(2)}, u32[]{:S(2)}) collective-permute-start(bf16[128,2048]{1,0:T(8,128)(2,1)S(1)} %get-tuple-element.8), channel_id=1, source_target_pairs={{0,256},{128,384},{256,0},{384,128},{1,257},{129,385},{257,1},{385... | collective-permute-start | bytes 1572872 | tf_op jit(solution)/shard_map/ppermute | solution.py:158
  53.0 47.1 %collective-permute-start.1 = (bf16[128,2048]{1,0:T(8,128)(2,1)S(1)}, bf16[128,2048]{1,0:T(8,128)(2,1)}, u32[]{:S(2)}, u32[]{:S(2)}) collective-permute-start(bf16[128,2048]{1,0:T(8,128)(2,1)S(1)} %get-tuple-element.6), channel_id=1, source_target_pairs={{0,128},{128,256},{256,384},{384,0},{1,129},{129,257},{257,385},{3... | collective-permute-start | bytes 1572872 | tf_op jit(solution)/shard_map/ppermute | solution.py:158
  55.6 5.4 %collective-permute-start = (s32[2,64]{1,0:T(2,128)S(1)}, s32[2,64]{1,0:T(2,128)S(1)}, u32[]{:S(2)}, u32[]{:S(2)}) collective-permute-start(s32[2,64]{1,0:T(2,128)S(1)} %fusion.2), channel_id=1, source_target_pairs={{0,1},{1,0},{2,3},{3,2},{4,5},{5,4},{6,7},{7,6},{8,9},{9,8},{10,11... | collective-permute-start | bytes 1544 | tf_op jit(solution)/shard_map/ppermute | solution.py:165
  72.5 27.6 %copy-start.1 = (bf16[128,2048]{1,0:T(8,128)(2,1)}, bf16[128,2048]{1,0:T(8,128)(2,1)S(1)}, u32[]{:S(2)}) copy-start(bf16[128,2048]{1,0:T(8,128)(2,1)S(1)} %collective-permute-done.3) | copy-start | bytes 1572868

commit v4 on v2

--- a/solution.py
+++ b/solution.py
@@ -15,29 +15,34 @@
 prior_weight = 1.0
 
 
-def place_kernel(slot_ref, scales_ref, grads_hbm, out_hbm, grads, placed, match, squares, in_sems, out_sems):
+def place_kernel(slot_hbm, scales_hbm, grads_hbm, out_hbm, slot_ref, scales_ref, grads, placed, match, squares, sems, out_sems):
     parts, count, quarter = grads.shape
     rows = match.shape[0]
     cols = quarter // SUB
-    copies_in = []
+    copies_in = [
+        pltpu.make_async_copy(slot_hbm, slot_ref, sems.at[parts]),
+        pltpu.make_async_copy(scales_hbm, scales_ref, sems.at[parts + 1]),
+    ]
     for i in range(parts):
-        copy = pltpu.make_async_copy(
-            grads_hbm.at[:, i * quarter : (i + 1) * quarter], grads.at[i], in_sems.at[i]
+        copies_in.append(
+            pltpu.make_async_copy(grads_hbm.at[:, i * quarter : (i + 1) * quarter], grads.at[i], sems.at[i])
         )
+    for copy in copies_in:
         copy.start()
-        copies_in.append(copy)
+    copies_in[0].wait()
     slot = slot_ref[...]
     for b in range(SUB):
         target = (slot // CAP) * (CAP * SUB) + (slot % CAP) * SUB + b
         hit = lax.broadcasted_iota(jnp.int32, (rows, count), 0) == target
         match[:, b * count : (b + 1) * count] = jnp.where(hit, 1.0, 0.0).astype(jnp.bfloat16)
+    for copy in copies_in[1:]:
+        copy.wait()
     scales = scales_ref[...]
     blocks = scales.shape[0]
     scales = jnp.concatenate([scales, jnp.zeros((-blocks % BLK, count), jnp.float32)], axis=0).T
     per = cols // BLK
     copies_out = []
     for i in range(parts):
-        copies_in[i].wait()
         for j in range(SUB * per):
             at = i * SUB * per + j
             scaled = grads[i, :, j * BLK : (j + 1) * BLK].astype(jnp.float32) * scales[:, at : at + 1]
@@ -56,34 +61,46 @@
         copy.wait()
 
 
-def select_kernel(target_ref, out_ref):
-    hit = lax.broadcasted_iota(jnp.int32, out_ref.shape, 0) == target_ref[...]
-    out_ref[...] = jnp.where(hit, 1.0, 0.0).astype(jnp.bfloat16)
-
-
-def merge_kernel(me_ref, select_ref, arrived_hbm, tables_ref, out_ref, arrived, fisher, sems):
+def merge_kernel(me_ref, target_ref, arrived_hbm, tables_hbm, out_hbm, arrived, tables, select, numer, denom, out, sems, table_sems, out_sems):
     parts, depth, cols = arrived.shape
-    rows = out_ref.shape[0]
+    rows = out.shape[0]
     copies = []
     for k in range(parts):
         at = pl.multiple_of(lax.rem(me_ref[0] + (parts - k), parts) * depth, depth)
-        copy = pltpu.make_async_copy(arrived_hbm.at[pl.ds(at, depth)], arrived.at[k], sems.at[k])
-        copy.start()
-        copies.append(copy)
+        copies.append(
+            (
+                pltpu.make_async_copy(arrived_hbm.at[pl.ds(at, depth)], arrived.at[k], sems.at[k]),
+                pltpu.make_async_copy(tables_hbm.at[k], tables.at[k], table_sems.at[k]),
+            )
+        )
+        for copy in copies[k]:
+            copy.start()
+    hit = lax.broadcasted_iota(jnp.int32, select.shape, 0) == target_ref[...]
+    select[...] = jnp.where(hit, 1.0, 0.0).astype(jnp.bfloat16)
+    copies_out = []
     for k in range(parts):
-        copies[k].wait()
-        fisher[k] = jnp.dot(select_ref[...], arrived[k], preferred_element_type=jnp.float32)
-    for b in range(SUB):
-        at = slice(b * cols, (b + 1) * cols)
-        numer = denom = None
-        for k in range(parts):
-            weight = (fisher[k, b * rows : (b + 1) * rows] + prior_weight).astype(jnp.bfloat16)
+        for copy in copies[k]:
+            copy.wait()
+        fisher = jnp.dot(select[...], arrived[k], preferred_element_type=jnp.float32)
+        for b in range(SUB):
+            at = slice(b * cols, (b + 1) * cols)
+            weight = (fisher[b * rows : (b + 1) * rows] + prior_weight).astype(jnp.bfloat16)
             weight = weight.astype(jnp.float32)
-            term = (weight * tables_ref[k, :, at].astype(jnp.float32)).astype(jnp.bfloat16)
+            term = (weight * tables[k, :, at].astype(jnp.float32)).astype(jnp.bfloat16)
             term = term.astype(jnp.float32)
-            numer = term if numer is None else numer + term
-            denom = weight if denom is None else denom + weight
-        out_ref[:, at] = (numer / denom).astype(jnp.bfloat16)
+            if k == 0:
+                numer[:, at] = term
+                denom[:, at] = weight
+            elif k < parts - 1:
+                numer[:, at] += term
+                denom[:, at] += weight
+            else:
+                out[:, at] = ((numer[:, at] + term) / (denom[:, at] + weight)).astype(jnp.bfloat16)
+                copy = pltpu.make_async_copy(out.at[:, at], out_hbm.at[:, at], out_sems.at[b])
+                copy.start()
+                copies_out.append(copy)
+    for copy in copies_out:
+        copy.wait()
 
 
 def per_device(token_ids, grad_values, grad_scales, tables):
@@ -105,8 +122,10 @@
     )
     rank = jnp.sum((same & before).astype(jnp.int32), axis=0)
     slot = owner * CAP + rank
-    tag_slot = (lax.rem(owner, near) * far + lax.div(owner, near)) * CAP + rank
-    match = lax.broadcasted_iota(jnp.int32, (groups * CAP, count), 0) == tag_slot[None, :]
+    at = lax.broadcasted_iota(jnp.uint32, (groups * CAP, count), 0)
+    spot = at // CAP
+    spot = ((spot % far) * near + spot // far) * CAP + at % CAP
+    match = spot.astype(jnp.int32) == slot[None, :]
     row_tags = jnp.sum(jnp.where(match, lax.rem(token_ids, rows)[None, :], 0), axis=1)
     near_rows = lax.all_to_all(
         row_tags.reshape(near, far * CAP),
@@ -121,18 +140,20 @@
     buffer = pl.pallas_call(
         place_kernel,
         in_specs=[
-            pl.BlockSpec(memory_space=pltpu.VMEM),
-            pl.BlockSpec(memory_space=pltpu.VMEM),
-            pl.BlockSpec(memory_space=pltpu.HBM),
+            pl.BlockSpec(memory_space=pl.ANY),
+            pl.BlockSpec(memory_space=pl.ANY),
+            pl.BlockSpec(memory_space=pl.ANY),
         ],
         out_specs=pl.BlockSpec(memory_space=pltpu.HBM),
         out_shape=jax.ShapeDtypeStruct((ckpts * groups * chunk, cols), jnp.bfloat16),
         scratch_shapes=[
+            pltpu.VMEM((1, count), jnp.int32),
+            pltpu.VMEM((width // BLK, count), jnp.float32),
             pltpu.VMEM((ckpts, count, quarter), jnp.bfloat16),
             pltpu.VMEM((ckpts * groups * chunk, cols), jnp.bfloat16),
             pltpu.VMEM((groups * chunk, SUB * count), jnp.bfloat16),
             pltpu.VMEM((ckpts, SUB * count, cols), jnp.bfloat16),
-            pltpu.SemaphoreType.DMA((ckpts,)),
+            pltpu.SemaphoreType.DMA((ckpts + 2,)),
             pltpu.SemaphoreType.DMA((ckpts,)),
         ],
         compiler_params=pltpu.CompilerParams(vmem_limit_bytes=56 << 20),
@@ -176,31 +197,30 @@
         passed, (lax.rem(far - far_me, far), 0), (far, near * CAP)
     ).reshape(groups * CAP, 1)
     target = arrived_rows + rows * jnp.arange(SUB, dtype=jnp.int32)
-    select = pl.pallas_call(
-        select_kernel,
-        out_shape=jax.ShapeDtypeStruct((SUB * rows, groups * chunk), jnp.bfloat16),
-        compiler_params=pltpu.CompilerParams(vmem_limit_bytes=16 << 20),
-        name="select",
-    )(target.reshape(1, groups * chunk))
-
     return pl.pallas_call(
         merge_kernel,
         in_specs=[
             pl.BlockSpec(memory_space=pltpu.SMEM),
             pl.BlockSpec(memory_space=pltpu.VMEM),
-            pl.BlockSpec(memory_space=pltpu.HBM),
-            pl.BlockSpec(memory_space=pltpu.VMEM),
-        ],
-        out_specs=pl.BlockSpec(memory_space=pltpu.VMEM),
+            pl.BlockSpec(memory_space=pl.ANY),
+            pl.BlockSpec(memory_space=pl.ANY),
+        ],
+        out_specs=pl.BlockSpec(memory_space=pltpu.HBM),
         out_shape=jax.ShapeDtypeStruct((rows, quarter), jnp.bfloat16),
         scratch_shapes=[
             pltpu.VMEM((ckpts, groups * chunk, cols), jnp.bfloat16),
-            pltpu.VMEM((ckpts, SUB * rows, cols), jnp.float32),
+            pltpu.VMEM((ckpts, rows, quarter), jnp.bfloat16),
+            pltpu.VMEM((SUB * rows, groups * chunk), jnp.bfloat16),
+            pltpu.VMEM((rows, quarter), jnp.float32),
+            pltpu.VMEM((rows, quarter), jnp.float32),
+            pltpu.VMEM((rows, quarter), jnp.bfloat16),
             pltpu.SemaphoreType.DMA((ckpts,)),
+            pltpu.SemaphoreType.DMA((ckpts,)),
+            pltpu.SemaphoreType.DMA((SUB,)),
         ],
         compiler_params=pltpu.CompilerParams(vmem_limit_bytes=32 << 20),
         name="merge",
-    )(me.astype(jnp.int32)[None], select, arrived, held)
+    )(me.astype(jnp.int32)[None], target.reshape(1, groups * chunk), arrived, held)
 
 
 def solution(mesh):

time: 144 us -> 142 us (0.986)
  Pallas kernels: 13.1 us -> 11 us
  waiting for transfers between devices: 62.2 us -> 64.2 us
  starting transfers between devices: 61.9 us -> 60.2 us
    pallas_call x2 -> x1, Pallas kernels: 7.36 us -> 5.5 us  [per_device(): pl.pallas_call(place_kernel, in_specs=[pl.BlockSpec(memory_space=pl.ANY),...]
    all_to_all x1, waiting for transfers between devices: 0.59 us -> 2.25 us  [per_device(): lax.all_to_all(row_tags.reshape(near, far * CAP), 'vocab', split_axis=0,...]
    all_to_all x1, starting transfers between devices: 21.4 us -> 19.8 us  [per_device(): lax.all_to_all(buffer.reshape(ckpts * groups, chunk, cols), ('ckpt', 'voc...]
  transfers between devices with their start and end apart: 8 -> 8, of which waited for: 5 -> 5; matrix products, arithmetic and copies ran while one was open for 3% -> 3% of each run, Pallas kernels for 5% -> 4%
where the time goes in v4:
time: 142 us; the launch traced here: 141 us
  waiting for transfers between devices  64.2 us (45%)
  starting transfers between devices  60.2 us (42%)
  Pallas kernels  11 us (8%)
  local copies, waits for them, and re-layouts  2.98 us (2%)
  other arithmetic  2.67 us (2%)
    ppermute x3, waiting for transfers between devices, per_device(): lax.ppermute(piece, 'vocab', [(v, (v + groups - m * near) % groups) for v...  24.2 us
    all_to_all x1, waiting for transfers between devices, per_device(): lax.all_to_all(buffer.reshape(ckpts * groups, chunk, cols), ('ckpt', 'voc...  20 us
    all_to_all x1, starting transfers between devices, per_device(): lax.all_to_all(buffer.reshape(ckpts * groups, chunk, cols), ('ckpt', 'voc...  19.8 us
    ppermute x3, waiting for transfers between devices, per_device(): lax.ppermute(piece, 'ckpt', [(i, (i + k) % ckpts) for i in range(ckpts)])  17.8 us
    ppermute x3, starting transfers between devices, per_device(): lax.ppermute(piece, 'vocab', [(v, (v + groups - m * near) % groups) for v...  15.9 us
    ppermute x3, starting transfers between devices, per_device(): lax.ppermute(piece, 'ckpt', [(i, (i + k) % ckpts) for i in range(ckpts)])  14 us
    all_to_all x1, starting transfers between devices, per_device(): lax.all_to_all(row_tags.reshape(near, far * CAP), 'vocab', split_axis=0,...  10.6 us
    pallas_call x1, Pallas kernels, per_device(): pl.pallas_call(place_kernel, in_specs=[pl.BlockSpec(memory_space=pl.ANY),...  5.5 us
  transfers between devices with their start and end apart: 8, of which 5 were waited for; matrix products, arithmetic and copies ran while one was open for 3% of the time, Pallas kernels for 4%

profile of v4, /device:TPU:1, one launch (start us, length us, event | category | flops | bytes accessed | tf_op | source)
XLA Modules:
  0.0 141.3 jit_solution(1951177942232236203)
XLA Ops:
  0.0 0.7 compare_select_fusion.1
  0.7 0.1 convert_reduce_fusion
  0.8 0.0 copy-start.2
  0.8 0.2 select_reduce_fusion
  1.0 0.7 all_to_all.9
  1.7 10.6 %all-to-all-start = ((s32[32,1,8]{2,1,0:T(1,128)}), s32[32,1,8]{2,1,0:T(1,128)S(1)}, u32[]{:S(2)}, u32[]{:S(2)}) async-start(s32[32,1,8]{2,1,0:T(1,128)} %bitcast.1), calls=%async_computation | async-start | bytes 32768 | tf_op jit(solution)/shard_map/all_to_all | solution.py:130
  12.2 0.0 copy-done.2
  12.3 5.5 %place.1 = bf16[4096,512]{1,0:T(8,128)(2,1)} custom-call(s32[1,128]{1,0:T(1,128)} %bitcast.30, f32[64,128]{1,0:T(8,128)} %bitcast.28, bf16[128,8192]{1,0:T(8,128)(2,1)} %bitcast.26), custom_call_target="tpu_custom_call" | custom-call | tf_op jit(solution)/shard_map/place/pallas_call | solution.py:140
  17.8 2.2 %all-to-all-done = s32[32,1,8]{2,1,0:T(1,128)S(1)} async-done(((s32[32,1,8]{2,1,0:T(1,128)}), s32[32,1,8]{2,1,0:T(1,128)S(1)}, u32[]{:S(2)}, u32[]{:S(2)}) %all-to-all-start) | async-done | bytes 1056 | tf_op jit(solution)/shard_map/all_to_all | solution.py:130
  20.0 0.0 copy-start
  20.0 19.8 %all-to-all-start.1 = ((bf16[512,8,512]{2,1,0:T(8,128)(2,1)}), bf16[512,8,512]{2,1,0:T(8,128)(2,1)}, u32[]{:S(2)}, u32[]{:S(2)}) async-start(bf16[512,8,512]{2,1,0:T(8,128)(2,1)} %bitcast.25), calls=%async_computation.1 | async-start | bytes 8388608 | tf_op jit(solution)/shard_map/all_to_all | solution.py:163
  39.8 0.0 copy-done
  39.8 1.2 constant_dynamic-slice_fusion
  41.0 3.3 %collective-permute-start.3 = (bf16[128,2048]{1,0:T(8,128)(2,1)}, bf16[128,2048]{1,0:T(8,128)(2,1)S(1)}, u32[]{:S(2)}, u32[]{:S(2)}) collective-permute-start(bf16[128,2048]{1,0:T(8,128)(2,1)} %get-tuple-element.14), channel_id=1, source_target_pairs={{0,128},{128,256},{256,384},{384,0},{1,129},{129,257},{257,385},{3... | collective-permute-start | bytes 1572872 | tf_op jit(solution)/shard_map/ppermute | solution.py:180
  44.3 4.3 %collective-permute-start.4 = (bf16[128,2048]{1,0:T(8,128)(2,1)}, bf16[128,2048]{1,0:T(8,128)(2,1)}, u32[]{:S(2)}, u32[]{:S(2)}) collective-permute-start(bf16[128,2048]{1,0:T(8,128)(2,1)} %get-tuple-element.13), channel_id=1, source_target_pairs={{0,256},{128,384},{256,0},{384,128},{1,257},{129,385},{257,1},{385... | collective-permute-start | bytes 1572872 | tf_op jit(solution)/shard_map/ppermute | solution.py:180
  48.7 17.8 %collective-permute-done.3 = bf16[128,2048]{1,0:T(8,128)(2,1)S(1)} collective-permute-done((bf16[128,2048]{1,0:T(8,128)(2,1)}, bf16[128,2048]{1,0:T(8,128)(2,1)S(1)}, u32[]{:S(2)}, u32[]{:S(2)}) %collective-permute-start.3) | collective-permute-done | bytes 524320 | tf_op jit(solution)/shard_map/ppermute | solution.py:180
  66.4 0.0 copy-start.1
  66.4 6.4 %collective-permute-start.5 = (bf16[128,2048]{1,0:T(8,128)(2,1)S(1)}, bf16[128,2048]{1,0:T(8,128)(2,1)}, u32[]{:S(2)}, u32[]{:S(2)}) collective-permute-start(bf16[128,2048]{1,0:T(8,128)(2,1)S(1)} %get-tuple-element.10), channel_id=1, source_target_pairs={{0,384},{128,0},{256,128},{384,256},{1,385},{129,1},{257,129},{385... | collective-permute-start | bytes 1572872 | tf_op jit(solution)/shard_map/ppermute | solution.py:180
  72.9 0.1 copy.17
  73.0 0.1 copy.19
  73.0 0.1 reshape.66
  73.2 5.9 %collective-permute-start = (s32[1,64]{1,0:T(1,128)S(1)}, s32[1,64]{1,0:T(1,128)S(1)}, u32[]{:S(2)}, u32[]{:S(2)}) collective-permute-start(s32[1,64]{1,0:T(1,128)S(1)} %reshape.66), channel_id=1, source_target_pairs={{0,96},{1,97},{2,98},{3,99},{4,100},{5,101},{6,102},{7,103},{8,104... | collective-permute-start | bytes 776 | tf_op jit(solution)/shard_map/ppermute | solution.py:191
  79.1 0.1 copy.20
  79.2 0.1 reshape.67
  79.3 6.0 %collective-permute-start.1 = (s32[1,64]{1,0:T(1,128)S(1)}, s32[1,64]{1,0:T(1,128)S(1)}, u32[]{:S(2)}, u32[]{:S(2)}) collective-permute-start(s32[1,64]{1,0:T(1,128)S(1)} %reshape.67), channel_id=1, source_target_pairs={{0,64},{1,65},{2,66},{3,67},{4,68},{5,69},{6,70},{7,71},{8,72},{9,... | collective-permute-start | bytes 776 | tf_op jit(solution)/shard_map/ppermute | solution.py:191
  85.3 0.1 copy.21
  85.4 0.1 reshape.68
  85.5 3.9 %collective-permute-start.2 = (s32[1,64]{1,0:T(1,128)S(1)}, s32[1,64]{1,0:T(1,128)S(1)}, u32[]{:S(2)}, u32[]{:S(2)}) collective-permute-start(s32[1,64]{1,0:T(1,128)S(1)} %reshape.68), channel_id=1, source_target_pairs={{0,32},{1,33},{2,34},{3,35},{4,36},{5,37},{6,38},{7,39},{8,40},{9,... | collective-permute-start | bytes 776 | tf_op jit(solution)/shard_map/ppermute | solution.py:191
  89.5 0.1 copy.18
  89.6 0.1 reshape.65
  89.7 14.5 %collective-permute-done = s32[1,64]{1,0:T(1,128)S(1)} collective-permute-done((s32[1,64]{1,0:T(1,128)S(1)}, s32[1,64]{1,0:T(1,128)S(1)}, u32[]{:S(2)}, u32[]{:S(2)}) %collective-permute-start) | collective-permute-done | bytes 288 | tf_op jit(solution)/shard_map/ppermute | solution.py:191
  104.1 9.7 %collective-permute-done.1 = s32[1,64]{1,0:T(1,128)S(1)} collective-permute-done((s32[1,64]{1,0:T(1,128)S(1)}, s32[1,64]{1,0:T(1,128)S(1)}, u32[]{:S(2)}, u32[]{:S(2)}) %collective-permute-start.1) | collective-permute-done | bytes 288 | tf_op jit(solution)/shard_map/ppermute | solution.py:191
  113.9 0.0 collective-permute-done.2
  113.9 0.1 add.96
  114.0 0.1 broadcast_add_fusion
  114.1 0.1 add.100.target_ref
  114.2 0.0 collective-permute-done.4
  114.3 0.0 collective-permute-done.5
  114.3 0.0 copy-done.1
  114.3 1.6 %pad_maximum_fusion.tables_hbm = bf16[4,128,2048]{2,1,0:T(8,128)(2,1)S(1)} fusion(bf16[1,128,2048]{2,1,0:T(8,128)(2,1)} %bitcast.13, bf16[1,128,2048]{2,1,0:T(8,128)(2,1)} %bitcast.12, bf16[1,128,2048]{2,1,0:T(8,128)(2,1)} %bitcast.27, bf16[1,128,2048]{2,1,0:T(8,128)(2,1)S(1)} %get-tuple-element.11), kind=kLoop, calls=%fused_computation | loop fusion | flops 3145728 | bytes 4194304 | tf_op jit(solution)/shard_map/stack | solution.py:181
  115.9 20.0 %all-to-all-done.1 = bf16[512,8,512]{2,1,0:T(8,128)(2,1)} async-done(((bf16[512,8,512]{2,1,0:T(8,128)(2,1)}), bf16[512,8,512]{2,1,0:T(8,128)(2,1)}, u32[]{:S(2)}, u32[]{:S(2)}) %all-to-all-start.1) | async-done | bytes 4194336 | tf_op jit(solution)/shard_map/all_to_all | solution.py:163
  135.9 5.5 %merge.1 = bf16[128,2048]{1,0:T(8,128)(2,1)} custom-call(s32[1]{0:T(128)} %bitcast.me_ref, s32[1,1024]{1,0:T(1,128)S(1)} %add.100.target_ref, bf16[4096,512]{1,0:T(8,128)(2,1)} %bitcast.7.arrived_hbm, bf16[4,128,2048]{2,1,0:T(8,128)(2,1)S(1)} %pad_maximum_fusion.tables_hbm), custom_call_target="tpu_custom_call" | custom-call | tf_op jit(solution)/shard_map/merge/pallas_call | solution.py:200
  (6 shorter events, 0.1 us)
Async XLA Ops:
  0.8 11.5 %copy-start.2 = (s32[128]{0:T(128)}, s32[128]{0:T(128)S(1)}, u32[]{:S(2)}) copy-start(s32[128]{0:T(128)S(1)} %multiply_add_fusion) | copy-start | bytes 1540
  1.7 18.3 %all-to-all-start = ((s32[32,1,8]{2,1,0:T(1,128)}), s32[32,1,8]{2,1,0:T(1,128)S(1)}, u32[]{:S(2)}, u32[]{:S(2)}) async-start(s32[32,1,8]{2,1,0:T(1,128)} %bitcast.1), calls=%async_computation | async-start | bytes 32768 | tf_op jit(solution)/shard_map/all_to_all | solution.py:130
  20.0 19.8 %copy-start = (bf16[1,128,8192]{2,1,0:T(8,128)(2,1)S(1)}, bf16[1,128,8192]{2,1,0:T(8,128)(2,1)}, u32[]{:S(2)}) copy-start(bf16[1,128,8192]{2,1,0:T(8,128)(2,1)} %param.11) | copy-start | bytes 6291460
  20.0 115.9 %all-to-all-start.1 = ((bf16[512,8,512]{2,1,0:T(8,128)(2,1)}), bf16[512,8,512]{2,1,0:T(8,128)(2,1)}, u32[]{:S(2)}, u32[]{:S(2)}) async-start(bf16[512,8,512]{2,1,0:T(8,128)(2,1)} %bitcast.25), calls=%async_computation.1 | async-start | bytes 8388608 | tf_op jit(solution)/shard_map/all_to_all | solution.py:163
  41.0 25.4 %collective-permute-start.3 = (bf16[128,2048]{1,0:T(8,128)(2,1)}, bf16[128,2048]{1,0:T(8,128)(2,1)S(1)}, u32[]{:S(2)}, u32[]{:S(2)}) collective-permute-start(bf16[128,2048]{1,0:T(8,128)(2,1)} %get-tuple-element.14), channel_id=1, source_target_pairs={{0,128},{128,256},{256,384},{384,0},{1,129},{129,257},{257,385},{3... | collective-permute-start | bytes 1572872 | tf_op jit(solution)/shard_map/ppermute | solution.py:180
  44.3 70.0 %collective-permute-start.4 = (bf16[128,2048]{1,0:T(8,128)(2,1)}, bf16[128,2048]{1,0:T(8,128)(2,1)}, u32[]{:S(2)}, u32[]{:S(2)}) collective-permute-start(bf16[128,2048]{1,0:T(8,128)(2,1)} %get-tuple-element.13), channel_id=1, source_target_pairs={{0,256},{128,384},{256,0},{384,128},{1,257},{129,385},{257,1},{385... | collective-permute-start | bytes 1572872 | tf_op jit(solution)/shard_map/ppermute | solution.py:180
  66.4 47.8 %copy-start.1 = (bf16[128,2048]{1,0:T(8,128)(2,1)}, bf16[128,2048]{1,0:T(8,128)(2,1)S(1)}, u32[]{:S(2)}) copy-start(bf16[128,2048]{1,0:T(8,128)(2,1)S(1)} %collective-permute-done.3) | copy-start | bytes 1572868
  66.4 47.8 %collective-permute-start.5 = (bf16[128,2048]{1,0:T(8,128)(2,1)S(1)}, bf16[128,2048]{1,0:T(8,128)(2,1)}, u32[]{:S(2)}, u32[]{:S(2)}) collective-permute-start(bf16[128,2048]{1,0:T(8,128)(2,1)S(1)} %get-tuple-element.10), channel_id=1, source_target_pairs={{0,384},{128,0},{256,128},{384,256},{1,385},{129,1},{257,129},{385... | collective-permute-start | bytes 1572872 | tf_op jit(solution)/shard_map/ppermute | solution.py:180
  73.2 31.0 %collective-permute-start = (s32[1,64]{1,0:T(1,128)S(1)}, s32[1,64]{1,0:T(1,128)S(1)}, u32[]{:S(2)}, u32[]{:S(2)}) collective-permute-start(s32[1,64]{1,0:T(1,128)S(1)} %reshape.66), channel_id=1, source_target_pairs={{0,96},{1,97},{2,98},{3,99},{4,100},{5,101},{6,102},{7,103},{8,104... | collective-permute-start | bytes 776 | tf_op jit(solution)/shard_map/ppermute | solution.py:191
  79.3 34.6 %collective-permute-start.1 = (s32[1,64]{1,0:T(1,128)S(1)}, s32[1,64]{1,0:T(1,128)S(1)}, u32[]{:S(2)}, u32[]{:S(2)}) collective-permute-start(s32[1,64]{1,0:T(1,128)S(1)} %reshape.67), channel_id=1, source_target_pairs={{0,64},{1,65},{2,66},{3,67},{4,68},{5,69},{6,70},{7,71},{8,72},{9,... | collective-permute-start | bytes 776 | tf_op jit(solution)/shard_map/ppermute | solution.py:191
  85.5 28.4 %collective-permute-start.2 = (s32[1,64]{1,0:T(1,128)S(1)}, s32[1,64]{1,0:T(1,128)S(1)}, u32[]{:S(2)}, u32[]{:S(2)}) collective-permute-start(s32[1,64]{1,0:T(1,128)S(1)} %reshape.68), channel_id=1, source_target_pairs={{0,32},{1,33},{2,34},{3,35},{4,36},{5,37},{6,38},{7,39},{8,40},{9,... | collective-permute-start | bytes 776 | tf_op jit(solution)/shard_map/ppermute | solution.py:191

commit v5 on v4

--- a/solution.py
+++ b/solution.py
@@ -61,12 +61,15 @@
         copy.wait()
 
 
-def merge_kernel(me_ref, target_ref, arrived_hbm, tables_hbm, out_hbm, arrived, tables, select, numer, denom, out, sems, table_sems, out_sems):
+def merge_kernel(target_hbm, arrived_hbm, tables_hbm, out_hbm, target_ref, arrived, tables, select, numer, denom, out, sems, table_sems, out_sems):
     parts, depth, cols = arrived.shape
     rows = out.shape[0]
+    me = lax.axis_index("ckpt")
+    tags = pltpu.make_async_copy(target_hbm, target_ref, sems.at[parts])
+    tags.start()
     copies = []
     for k in range(parts):
-        at = pl.multiple_of(lax.rem(me_ref[0] + (parts - k), parts) * depth, depth)
+        at = pl.multiple_of(lax.rem(me + (parts - k), parts) * depth, depth)
         copies.append(
             (
                 pltpu.make_async_copy(arrived_hbm.at[pl.ds(at, depth)], arrived.at[k], sems.at[k]),
@@ -75,13 +78,14 @@
         )
         for copy in copies[k]:
             copy.start()
+    tags.wait()
     hit = lax.broadcasted_iota(jnp.int32, select.shape, 0) == target_ref[...]
     select[...] = jnp.where(hit, 1.0, 0.0).astype(jnp.bfloat16)
     copies_out = []
     for k in range(parts):
-        for copy in copies[k]:
-            copy.wait()
+        copies[k][0].wait()
         fisher = jnp.dot(select[...], arrived[k], preferred_element_type=jnp.float32)
+        copies[k][1].wait()
         for b in range(SUB):
             at = slice(b * cols, (b + 1) * cols)
             weight = (fisher[b * rows : (b + 1) * rows] + prior_weight).astype(jnp.bfloat16)
@@ -200,27 +204,27 @@
     return pl.pallas_call(
         merge_kernel,
         in_specs=[
-            pl.BlockSpec(memory_space=pltpu.SMEM),
-            pl.BlockSpec(memory_space=pltpu.VMEM),
+            pl.BlockSpec(memory_space=pl.ANY),
             pl.BlockSpec(memory_space=pl.ANY),
             pl.BlockSpec(memory_space=pl.ANY),
         ],
         out_specs=pl.BlockSpec(memory_space=pltpu.HBM),
         out_shape=jax.ShapeDtypeStruct((rows, quarter), jnp.bfloat16),
         scratch_shapes=[
+            pltpu.VMEM((1, groups * chunk), jnp.int32),
             pltpu.VMEM((ckpts, groups * chunk, cols), jnp.bfloat16),
             pltpu.VMEM((ckpts, rows, quarter), jnp.bfloat16),
             pltpu.VMEM((SUB * rows, groups * chunk), jnp.bfloat16),
             pltpu.VMEM((rows, quarter), jnp.float32),
             pltpu.VMEM((rows, quarter), jnp.float32),
             pltpu.VMEM((rows, quarter), jnp.bfloat16),
-            pltpu.SemaphoreType.DMA((ckpts,)),
+            pltpu.SemaphoreType.DMA((ckpts + 1,)),
             pltpu.SemaphoreType.DMA((ckpts,)),
             pltpu.SemaphoreType.DMA((SUB,)),
         ],
         compiler_params=pltpu.CompilerParams(vmem_limit_bytes=32 << 20),
         name="merge",
-    )(me.astype(jnp.int32)[None], target.reshape(1, groups * chunk), arrived, held)
+    )(target.reshape(1, groups * chunk), arrived, held)
 
 
 def solution(mesh):

time: 142 us -> 143 us (level)
  no operation moved by 1% of the time
where the time goes in v5:
time: 143 us; the launch traced here: 142 us
  waiting for transfers between devices  64.2 us (45%)
  starting transfers between devices  60.2 us (42%)
  Pallas kernels  11.8 us (8%)
  local copies, waits for them, and re-layouts  2.98 us (2%)
  other arithmetic  2.67 us (2%)
    ppermute x3, waiting for transfers between devices, per_device(): lax.ppermute(piece, 'vocab', [(v, (v + groups - m * near) % groups) for v...  24.2 us
    all_to_all x1, waiting for transfers between devices, per_device(): lax.all_to_all(buffer.reshape(ckpts * groups, chunk, cols), ('ckpt', 'voc...  20 us
    all_to_all x1, starting transfers between devices, per_device(): lax.all_to_all(buffer.reshape(ckpts * groups, chunk, cols), ('ckpt', 'voc...  19.8 us
    ppermute x3, waiting for transfers between devices, per_device(): lax.ppermute(piece, 'ckpt', [(i, (i + k) % ckpts) for i in range(ckpts)])  17.8 us
    ppermute x3, starting transfers between devices, per_device(): lax.ppermute(piece, 'vocab', [(v, (v + groups - m * near) % groups) for v...  15.9 us
    ppermute x3, starting transfers between devices, per_device(): lax.ppermute(piece, 'ckpt', [(i, (i + k) % ckpts) for i in range(ckpts)])  14 us
    all_to_all x1, starting transfers between devices, per_device(): lax.all_to_all(row_tags.reshape(near, far * CAP), 'vocab', split_axis=0,...  10.6 us
    pallas_call x1, Pallas kernels, per_device(): pl.pallas_call(merge_kernel, in_specs=[pl.BlockSpec(memory_space=pl.ANY),...  6.27 us
  transfers between devices with their start and end apart: 8, of which 5 were waited for; matrix products, arithmetic and copies ran while one was open for 3% of the time, Pallas kernels for 4%

profile of v5, /device:TPU:1, one launch (start us, length us, event | category | flops | bytes accessed | tf_op | source)
XLA Modules:
  0.0 142.2 jit_solution(8710477308653278843)
XLA Ops:
  0.0 0.7 compare_select_fusion.1
  0.7 0.1 convert_reduce_fusion
  0.8 0.0 copy-start.2
  0.8 0.2 select_reduce_fusion
  1.0 0.7 all_to_all.9
  1.7 10.6 %all-to-all-start = ((s32[32,1,8]{2,1,0:T(1,128)}), s32[32,1,8]{2,1,0:T(1,128)S(1)}, u32[]{:S(2)}, u32[]{:S(2)}) async-start(s32[32,1,8]{2,1,0:T(1,128)} %bitcast), calls=%async_computation | async-start | bytes 32768 | tf_op jit(solution)/shard_map/all_to_all | solution.py:134
  12.2 0.0 copy-done.2
  12.3 5.5 %place.1 = bf16[4096,512]{1,0:T(8,128)(2,1)} custom-call(s32[1,128]{1,0:T(1,128)} %bitcast.29, f32[64,128]{1,0:T(8,128)} %bitcast.27, bf16[128,8192]{1,0:T(8,128)(2,1)} %bitcast.25), custom_call_target="tpu_custom_call" | custom-call | tf_op jit(solution)/shard_map/place/pallas_call | solution.py:144
  17.8 2.2 %all-to-all-done = s32[32,1,8]{2,1,0:T(1,128)S(1)} async-done(((s32[32,1,8]{2,1,0:T(1,128)}), s32[32,1,8]{2,1,0:T(1,128)S(1)}, u32[]{:S(2)}, u32[]{:S(2)}) %all-to-all-start) | async-done | bytes 1056 | tf_op jit(solution)/shard_map/all_to_all | solution.py:134
  20.0 0.0 copy-start
  20.0 19.8 %all-to-all-start.1 = ((bf16[512,8,512]{2,1,0:T(8,128)(2,1)}), bf16[512,8,512]{2,1,0:T(8,128)(2,1)}, u32[]{:S(2)}, u32[]{:S(2)}) async-start(bf16[512,8,512]{2,1,0:T(8,128)(2,1)} %bitcast.24), calls=%async_computation.1 | async-start | bytes 8388608 | tf_op jit(solution)/shard_map/all_to_all | solution.py:167
  39.8 0.0 copy-done
  39.8 1.2 constant_dynamic-slice_fusion
  41.0 3.3 %collective-permute-start.3 = (bf16[128,2048]{1,0:T(8,128)(2,1)}, bf16[128,2048]{1,0:T(8,128)(2,1)S(1)}, u32[]{:S(2)}, u32[]{:S(2)}) collective-permute-start(bf16[128,2048]{1,0:T(8,128)(2,1)} %get-tuple-element.14), channel_id=1, source_target_pairs={{0,128},{128,256},{256,384},{384,0},{1,129},{129,257},{257,385},{3... | collective-permute-start | bytes 1572872 | tf_op jit(solution)/shard_map/ppermute | solution.py:184
  44.3 4.3 %collective-permute-start.4 = (bf16[128,2048]{1,0:T(8,128)(2,1)}, bf16[128,2048]{1,0:T(8,128)(2,1)}, u32[]{:S(2)}, u32[]{:S(2)}) collective-permute-start(bf16[128,2048]{1,0:T(8,128)(2,1)} %get-tuple-element.13), channel_id=1, source_target_pairs={{0,256},{128,384},{256,0},{384,128},{1,257},{129,385},{257,1},{385... | collective-permute-start | bytes 1572872 | tf_op jit(solution)/shard_map/ppermute | solution.py:184
  48.7 17.8 %collective-permute-done.3 = bf16[128,2048]{1,0:T(8,128)(2,1)S(1)} collective-permute-done((bf16[128,2048]{1,0:T(8,128)(2,1)}, bf16[128,2048]{1,0:T(8,128)(2,1)S(1)}, u32[]{:S(2)}, u32[]{:S(2)}) %collective-permute-start.3) | collective-permute-done | bytes 524320 | tf_op jit(solution)/shard_map/ppermute | solution.py:184
  66.4 0.0 copy-start.1
  66.4 6.4 %collective-permute-start.5 = (bf16[128,2048]{1,0:T(8,128)(2,1)S(1)}, bf16[128,2048]{1,0:T(8,128)(2,1)}, u32[]{:S(2)}, u32[]{:S(2)}) collective-permute-start(bf16[128,2048]{1,0:T(8,128)(2,1)S(1)} %get-tuple-element.10), channel_id=1, source_target_pairs={{0,384},{128,0},{256,128},{384,256},{1,385},{129,1},{257,129},{385... | collective-permute-start | bytes 1572872 | tf_op jit(solution)/shard_map/ppermute | solution.py:184
  72.9 0.1 copy.17
  73.0 0.1 copy.19
  73.0 0.1 reshape.66
  73.2 5.9 %collective-permute-start = (s32[1,64]{1,0:T(1,128)S(1)}, s32[1,64]{1,0:T(1,128)S(1)}, u32[]{:S(2)}, u32[]{:S(2)}) collective-permute-start(s32[1,64]{1,0:T(1,128)S(1)} %reshape.66), channel_id=1, source_target_pairs={{0,96},{1,97},{2,98},{3,99},{4,100},{5,101},{6,102},{7,103},{8,104... | collective-permute-start | bytes 776 | tf_op jit(solution)/shard_map/ppermute | solution.py:195
  79.1 0.1 copy.20
  79.2 0.1 reshape.67
  79.3 6.0 %collective-permute-start.1 = (s32[1,64]{1,0:T(1,128)S(1)}, s32[1,64]{1,0:T(1,128)S(1)}, u32[]{:S(2)}, u32[]{:S(2)}) collective-permute-start(s32[1,64]{1,0:T(1,128)S(1)} %reshape.67), channel_id=1, source_target_pairs={{0,64},{1,65},{2,66},{3,67},{4,68},{5,69},{6,70},{7,71},{8,72},{9,... | collective-permute-start | bytes 776 | tf_op jit(solution)/shard_map/ppermute | solution.py:195
  85.3 0.1 copy.21
  85.4 0.1 reshape.68
  85.5 3.9 %collective-permute-start.2 = (s32[1,64]{1,0:T(1,128)S(1)}, s32[1,64]{1,0:T(1,128)S(1)}, u32[]{:S(2)}, u32[]{:S(2)}) collective-permute-start(s32[1,64]{1,0:T(1,128)S(1)} %reshape.68), channel_id=1, source_target_pairs={{0,32},{1,33},{2,34},{3,35},{4,36},{5,37},{6,38},{7,39},{8,40},{9,... | collective-permute-start | bytes 776 | tf_op jit(solution)/shard_map/ppermute | solution.py:195
  89.5 0.1 copy.18
  89.6 0.1 reshape.65
  89.7 14.5 %collective-permute-done = s32[1,64]{1,0:T(1,128)S(1)} collective-permute-done((s32[1,64]{1,0:T(1,128)S(1)}, s32[1,64]{1,0:T(1,128)S(1)}, u32[]{:S(2)}, u32[]{:S(2)}) %collective-permute-start) | collective-permute-done | bytes 288 | tf_op jit(solution)/shard_map/ppermute | solution.py:195
  104.1 9.7 %collective-permute-done.1 = s32[1,64]{1,0:T(1,128)S(1)} collective-permute-done((s32[1,64]{1,0:T(1,128)S(1)}, s32[1,64]{1,0:T(1,128)S(1)}, u32[]{:S(2)}, u32[]{:S(2)}) %collective-permute-start.1) | collective-permute-done | bytes 288 | tf_op jit(solution)/shard_map/ppermute | solution.py:195
  113.9 0.0 collective-permute-done.2
  113.9 0.1 add.96
  114.0 0.1 broadcast_add_fusion
  114.1 0.1 add.100.target_hbm
  114.2 0.0 collective-permute-done.4
  114.3 0.0 collective-permute-done.5
  114.3 0.0 copy-done.1
  114.3 1.6 %pad_maximum_fusion.tables_hbm = bf16[4,128,2048]{2,1,0:T(8,128)(2,1)S(1)} fusion(bf16[1,128,2048]{2,1,0:T(8,128)(2,1)} %bitcast.12, bf16[1,128,2048]{2,1,0:T(8,128)(2,1)} %bitcast.11, bf16[1,128,2048]{2,1,0:T(8,128)(2,1)} %bitcast.26, bf16[1,128,2048]{2,1,0:T(8,128)(2,1)S(1)} %get-tuple-element.11), kind=kLoop, calls=%fused_computation | loop fusion | flops 3145728 | bytes 4194304 | tf_op jit(solution)/shard_map/stack | solution.py:185
  115.9 20.0 %all-to-all-done.1 = bf16[512,8,512]{2,1,0:T(8,128)(2,1)} async-done(((bf16[512,8,512]{2,1,0:T(8,128)(2,1)}), bf16[512,8,512]{2,1,0:T(8,128)(2,1)}, u32[]{:S(2)}, u32[]{:S(2)}) %all-to-all-start.1) | async-done | bytes 4194336 | tf_op jit(solution)/shard_map/all_to_all | solution.py:167
  135.9 6.3 %merge.1 = bf16[128,2048]{1,0:T(8,128)(2,1)} custom-call(s32[1,1024]{1,0:T(1,128)S(1)} %add.100.target_hbm, bf16[4096,512]{1,0:T(8,128)(2,1)} %bitcast.6.arrived_hbm, bf16[4,128,2048]{2,1,0:T(8,128)(2,1)S(1)} %pad_maximum_fusion.tables_hbm), custom_call_target="tpu_custom_call" | custom-call | tf_op jit(solution)/shard_map/merge/pallas_call | solution.py:204
  (6 shorter events, 0.1 us)
Async XLA Ops:
  0.8 11.5 %copy-start.2 = (s32[128]{0:T(128)}, s32[128]{0:T(128)S(1)}, u32[]{:S(2)}) copy-start(s32[128]{0:T(128)S(1)} %multiply_add_fusion) | copy-start | bytes 1540
  1.7 18.3 %all-to-all-start = ((s32[32,1,8]{2,1,0:T(1,128)}), s32[32,1,8]{2,1,0:T(1,128)S(1)}, u32[]{:S(2)}, u32[]{:S(2)}) async-start(s32[32,1,8]{2,1,0:T(1,128)} %bitcast), calls=%async_computation | async-start | bytes 32768 | tf_op jit(solution)/shard_map/all_to_all | solution.py:134
  20.0 19.8 %copy-start = (bf16[1,128,8192]{2,1,0:T(8,128)(2,1)S(1)}, bf16[1,128,8192]{2,1,0:T(8,128)(2,1)}, u32[]{:S(2)}) copy-start(bf16[1,128,8192]{2,1,0:T(8,128)(2,1)} %param.11) | copy-start | bytes 6291460
  20.0 115.9 %all-to-all-start.1 = ((bf16[512,8,512]{2,1,0:T(8,128)(2,1)}), bf16[512,8,512]{2,1,0:T(8,128)(2,1)}, u32[]{:S(2)}, u32[]{:S(2)}) async-start(bf16[512,8,512]{2,1,0:T(8,128)(2,1)} %bitcast.24), calls=%async_computation.1 | async-start | bytes 8388608 | tf_op jit(solution)/shard_map/all_to_all | solution.py:167
  41.0 25.4 %collective-permute-start.3 = (bf16[128,2048]{1,0:T(8,128)(2,1)}, bf16[128,2048]{1,0:T(8,128)(2,1)S(1)}, u32[]{:S(2)}, u32[]{:S(2)}) collective-permute-start(bf16[128,2048]{1,0:T(8,128)(2,1)} %get-tuple-element.14), channel_id=1, source_target_pairs={{0,128},{128,256},{256,384},{384,0},{1,129},{129,257},{257,385},{3... | collective-permute-start | bytes 1572872 | tf_op jit(solution)/shard_map/ppermute | solution.py:184
  44.3 70.0 %collective-permute-start.4 = (bf16[128,2048]{1,0:T(8,128)(2,1)}, bf16[128,2048]{1,0:T(8,128)(2,1)}, u32[]{:S(2)}, u32[]{:S(2)}) collective-permute-start(bf16[128,2048]{1,0:T(8,128)(2,1)} %get-tuple-element.13), channel_id=1, source_target_pairs={{0,256},{128,384},{256,0},{384,128},{1,257},{129,385},{257,1},{385... | collective-permute-start | bytes 1572872 | tf_op jit(solution)/shard_map/ppermute | solution.py:184
  66.4 47.8 %copy-start.1 = (bf16[128,2048]{1,0:T(8,128)(2,1)}, bf16[128,2048]{1,0:T(8,128)(2,1)S(1)}, u32[]{:S(2)}) copy-start(bf16[128,2048]{1,0:T(8,128)(2,1)S(1)} %collective-permute-done.3) | copy-start | bytes 1572868
  66.4 47.8 %collective-permute-start.5 = (bf16[128,2048]{1,0:T(8,128)(2,1)S(1)}, bf16[128,2048]{1,0:T(8,128)(2,1)}, u32[]{:S(2)}, u32[]{:S(2)}) collective-permute-start(bf16[128,2048]{1,0:T(8,128)(2,1)S(1)} %get-tuple-element.10), channel_id=1, source_target_pairs={{0,384},{128,0},{256,128},{384,256},{1,385},{129,1},{257,129},{385... | collective-permute-start | bytes 1572872 | tf_op jit(solution)/shard_map/ppermute | solution.py:184
  73.2 31.0 %collective-permute-start = (s32[1,64]{1,0:T(1,128)S(1)}, s32[1,64]{1,0:T(1,128)S(1)}, u32[]{:S(2)}, u32[]{:S(2)}) collective-permute-start(s32[1,64]{1,0:T(1,128)S(1)} %reshape.66), channel_id=1, source_target_pairs={{0,96},{1,97},{2,98},{3,99},{4,100},{5,101},{6,102},{7,103},{8,104... | collective-permute-start | bytes 776 | tf_op jit(solution)/shard_map/ppermute | solution.py:195
  79.3 34.6 %collective-permute-start.1 = (s32[1,64]{1,0:T(1,128)S(1)}, s32[1,64]{1,0:T(1,128)S(1)}, u32[]{:S(2)}, u32[]{:S(2)}) collective-permute-start(s32[1,64]{1,0:T(1,128)S(1)} %reshape.67), channel_id=1, source_target_pairs={{0,64},{1,65},{2,66},{3,67},{4,68},{5,69},{6,70},{7,71},{8,72},{9,... | collective-permute-start | bytes 776 | tf_op jit(solution)/shard_map/ppermute | solution.py:195
  85.5 28.4 %collective-permute-start.2 = (s32[1,64]{1,0:T(1,128)S(1)}, s32[1,64]{1,0:T(1,128)S(1)}, u32[]{:S(2)}, u32[]{:S(2)}) collective-permute-start(s32[1,64]{1,0:T(1,128)S(1)} %reshape.68), channel_id=1, source_target_pairs={{0,32},{1,33},{2,34},{3,35},{4,36},{5,37},{6,38},{7,39},{8,40},{9,... | collective-permute-start | bytes 776 | tf_op jit(solution)/shard_map/ppermute | solution.py:195
